TPU v7x, 128 devices: a whole 4x4x4 slice. The times are simulated.
128 devices in a mesh: snap: 4 (over y), vert: 32 (over z, x, core).
Axes of the slice: x: 4, y: 4, z: 4, core: 2. Of those that a mesh axis runs over, the one named last changes fastest.
Arguments:
- features: bfloat16 [32, 8192, 256], P('snap', 'vert'), may hold values from -6 to 6
- tile_cols: int32 [32, 64, 4], P('snap', 'vert'), may hold values from -1 to 63, as said below
- counts: int32 [32, 64], P('snap', 'vert'), may hold values from 1 to 4
- birth_snap: int32 [8192], P('vert'), may hold values from 0 to 31
- query_proj: bfloat16 [256, 256], replicated, may hold values from -0.375 to 0.375
- keyval_proj: bfloat16 [256, 512], replicated, may hold values from -0.375 to 0.375
- struct_out: bfloat16 [256, 256], replicated, may hold values from -0.375 to 0.375
- position_embedding_table: bfloat16 [32, 256], replicated, may hold values from -3 to 3
- temporal_qkv_weight: bfloat16 [256, 768], replicated, may hold values from -0.375 to 0.375
- temporal_output_weight: bfloat16 [256, 256], replicated, may hold values from -0.375 to 0.375
Outputs:
- embeddings: float32 [32, 32, 4, 64, 256], P(None, 'vert', 'snap')
Inputs may be any that keep to these rules, and one draw needn't show every extreme that they name: `tile_cols`: entries k < counts[s, r] name column blocks of occupied tiles (a block may appear twice); the others are -1. Of the live entries of the 8 x 2 row blocks of one device, at most 3 lie in column blocks of any one index of vert, and exactly 3 for one index.
All inputs are finite; a program needn't handle non-finite values.
Results may differ from a plain program's by a relative error of at most 0.008.
Values may be sent and summed in bfloat16 or wider, within the bound.
A program may use at most 128 MiB of HBM per device.

v0:
```python
import jax
import jax.numpy as jnp
from jax import lax
from jax.sharding import PartitionSpec as P

HEADS = 8
TILE = 128


def head_columns(model_width):
    head_size = model_width // HEADS
    column_head = jnp.arange(model_width, dtype=jnp.int32)[None, :] // head_size
    return (column_head == jnp.arange(HEADS, dtype=jnp.int32)[:, None]).astype(jnp.bfloat16)


def widen_heads(rows, column_mask):
    count, length, model_width = rows.shape
    spread = rows[:, None, :, :] * column_mask[None, :, None, :]
    return spread.reshape(count, HEADS * length, model_width)


def attend_tiles(query_rows_all, key_rows, live_keys):
    count, span, model_width = query_rows_all.shape
    head_size = model_width // HEADS
    length = key_rows.shape[1]
    column_mask = head_columns(model_width)
    widened_keys = widen_heads(key_rows[:, :, :model_width], column_mask)
    widened_values = widen_heads(key_rows[:, :, model_width:], column_mask)
    scores = jnp.einsum(
        "twn,thn->twh", query_rows_all, widened_keys, preferred_element_type=jnp.float32
    ) * head_size ** (-0.5)
    scores = scores.reshape(count, span, HEADS, length)
    scores = jnp.where(live_keys[:, None, None, :], scores, -jnp.inf)
    weight_matrices = (
        jax.nn.softmax(scores, axis=-1).astype(jnp.bfloat16).reshape(count, span, HEADS * length)
    )
    blended_rows = jnp.einsum(
        "gyv,gvl->gyl", weight_matrices, widened_values, preferred_element_type=jnp.float32
    )
    return blended_rows.astype(jnp.bfloat16)


def time_layer(
    hidden_block, births, position_embedding_table, temporal_qkv_weight, temporal_output_weight
):
    length, count, model_width = hidden_block.shape
    head_size = model_width // HEADS
    vertex_rows = jnp.transpose(hidden_block, (1, 0, 2))
    blended_input = (
        vertex_rows.astype(jnp.float32) + position_embedding_table.astype(jnp.float32)[None, :, :]
    ).astype(jnp.bfloat16)
    projected_rows = jnp.einsum(
        "csf,fz->csz", blended_input, temporal_qkv_weight, preferred_element_type=jnp.float32
    ).astype(jnp.bfloat16)
    column_mask = head_columns(model_width)
    query_rows_all = projected_rows[:, :, :model_width]
    widened_keys = widen_heads(projected_rows[:, :, model_width : 2 * model_width], column_mask)
    widened_values = widen_heads(projected_rows[:, :, 2 * model_width :], column_mask)
    scores = jnp.einsum(
        "csd,cxd->csx", query_rows_all, widened_keys, preferred_element_type=jnp.float32
    ) * head_size ** (-0.5)
    scores = scores.reshape(count, length, HEADS, length)
    later = jnp.arange(length, dtype=jnp.int32)[:, None]
    earlier = jnp.arange(length, dtype=jnp.int32)[None, :]
    allowed = (earlier <= later)[None] & (earlier[None] >= births[:, None, None]) | (
        earlier == later
    )[None]
    scores = jnp.where(allowed[:, :, None, :], scores, -jnp.inf)
    weight_matrices = (
        jax.nn.softmax(scores, axis=-1).astype(jnp.bfloat16).reshape(count, length, HEADS * length)
    )
    blended_rows = jnp.einsum(
        "csx,cxd->csd", weight_matrices, widened_values, preferred_element_type=jnp.float32
    ).astype(jnp.bfloat16)
    update_rows = jnp.einsum(
        "csf,fz->csz", blended_rows, temporal_output_weight, preferred_element_type=jnp.float32
    )
    result_rows = vertex_rows.astype(jnp.float32) + update_rows
    return jnp.transpose(result_rows, (1, 0, 2))


def local(
    features,
    tile_cols,
    counts,
    birth_snap,
    query_proj,
    keyval_proj,
    struct_out,
    position_embedding_table,
    temporal_qkv_weight,
    temporal_output_weight,
):
    snap_count, vert_rows, model_width = features.shape
    blocks = vert_rows // TILE
    tile_slots = tile_cols.shape[2]
    peer_count = lax.axis_size("vert")
    capacity = max(2, (snap_count * blocks * tile_slots + peer_count - 2) // (peer_count - 1))
    flat_rows = features.reshape(snap_count * vert_rows, model_width)
    query_rows_all = jnp.dot(flat_rows, query_proj, preferred_element_type=jnp.float32).astype(
        jnp.bfloat16
    )
    query_rows_all = query_rows_all.reshape(snap_count, blocks, TILE, model_width)
    live_tiles = jnp.arange(tile_slots, dtype=jnp.int32)[None, None, :] < counts[:, :, None]
    owning_devices = tile_cols // blocks
    block_codes = (
        jnp.arange(snap_count, dtype=jnp.int32)[:, None, None] * blocks + tile_cols % blocks
    )
    live_flat = live_tiles.reshape(-1)
    owners_flat = owning_devices.reshape(-1)
    onehot = (
        (owners_flat[:, None] == jnp.arange(peer_count, dtype=jnp.int32)[None, :])
        & live_flat[:, None]
    ).astype(jnp.int32)
    slot_rank = jnp.sum((jnp.cumsum(onehot, axis=0) - onehot) * onehot, axis=1)
    slot_index = jnp.where(live_flat, owners_flat * capacity + slot_rank, peer_count * capacity)
    outgoing_codes = (
        jnp.full((peer_count * capacity,), -1, jnp.int32)
        .at[slot_index]
        .set(block_codes.reshape(-1), mode="drop")
    )
    requested_tiles = lax.all_to_all(
        outgoing_codes.reshape(peer_count, capacity),
        "vert",
        split_axis=0,
        concat_axis=0,
        tiled=True,
    )
    picked = jnp.clip(requested_tiles.reshape(-1), 0, snap_count * blocks - 1)
    feature_blocks = features.reshape(snap_count * blocks, TILE, model_width)
    outgoing = feature_blocks[picked].reshape(peer_count, capacity, TILE, model_width)
    incoming = lax.all_to_all(outgoing, "vert", split_axis=0, concat_axis=0, tiled=True)
    fetched = jnp.dot(
        incoming.reshape(-1, model_width), keyval_proj, preferred_element_type=jnp.float32
    )
    fetched = fetched.astype(jnp.bfloat16).reshape(peer_count * capacity, TILE, 2 * model_width)
    slot_table = jnp.where(live_tiles, slot_index.reshape(snap_count, blocks, tile_slots), 0)

    def per_snapshot(pieces):
        query_block, slot_block, live_block = pieces
        key_rows = fetched[slot_block].reshape(blocks, tile_slots * TILE, 2 * model_width)
        live_keys = jnp.repeat(live_block, TILE, axis=1)
        return attend_tiles(query_block, key_rows, live_keys)

    attended = lax.map(per_snapshot, (query_rows_all, slot_table, live_tiles)).reshape(
        snap_count * vert_rows, model_width
    )
    update_rows = jnp.dot(attended, struct_out, preferred_element_type=jnp.float32)
    hidden = (
        (flat_rows.astype(jnp.float32) + update_rows)
        .astype(jnp.bfloat16)
        .reshape(snap_count, vert_rows, model_width)
    )
    groups = lax.axis_size("snap")
    quarter = vert_rows // groups
    split_rows = hidden.reshape(snap_count, groups, quarter, model_width)
    arrived = lax.all_to_all(split_rows, "snap", split_axis=1, concat_axis=0, tiled=True)
    born_at = lax.dynamic_slice_in_dim(birth_snap, lax.axis_index("snap") * quarter, quarter)
    result = time_layer(
        arrived[:, 0],
        born_at,
        position_embedding_table,
        temporal_qkv_weight,
        temporal_output_weight,
    )[:, None]
    return result[:, None]


def solution(mesh):
    placed = (
        P("snap", "vert", None),
        P("snap", "vert", None),
        P("snap", "vert"),
        P("vert"),
        P(),
        P(),
        P(),
        P(),
        P(),
        P(),
    )
    return jax.shard_map(
        local,
        mesh=mesh,
        in_specs=placed,
        out_specs=P(None, "vert", "snap", None, None),
        check_vma=False,
    )
```

profile of v0, /device:TPU:0, one launch (start us, length us, event | category | flops | bytes accessed | tf_op | source)
XLA Modules:
  0.0 488.2 jit_solution(4414794597096327159)
XLA Ops:
  3.5 15.4 %all_to_all.23 = s32[32,1,3]{2,1,0:T(1,128)S(1)} all-to-all(s32[32,1,3]{2,1,0:T(1,128)S(1)} %bitcast.164), channel_id=1, replica_groups=mesh['snap'=4,'vert'=32] {'vert'}, dimensions={0} | all-to-all | bytes 768 | tf_op jit(solution)/shard_map/all_to_all | solution.py:122
  19.1 7.2 %gather_fusion.1 = bf16[96,128,256]{2,1,0:T(8,128)(2,1)} fusion(bf16[16,128,256]{2,1,0:T(8,128)(2,1)} %bitcast.147, s32[1024]{0:T(1024)S(1)} %pad_clamp_fusion.1), kind=kCustom, calls=%fused_computation.1 | custom fusion | bytes 12583296 | tf_op jit(solution)/shard_map/gather | solution.py:131
  26.3 5.0 %all-to-all-start.1 = ((bf16[32,3,128,256]{3,2,1,0:T(8,128)(2,1)}), bf16[32,3,128,256]{3,2,1,0:T(8,128)(2,1)}, u32[]{:S(2)}, u32[]{:S(2)}) async-start(bf16[32,3,128,256]{3,2,1,0:T(8,128)(2,1)} %bitcast.152), calls=%async_computation.1 | async-start | bytes 12582912 | tf_op jit(solution)/shard_map/all_to_all | solution.py:132
  33.8 75.4 %all-to-all-done.1 = bf16[32,3,128,256]{3,2,1,0:T(8,128)(2,1)} async-done(((bf16[32,3,128,256]{3,2,1,0:T(8,128)(2,1)}), bf16[32,3,128,256]{3,2,1,0:T(8,128)(2,1)}, u32[]{:S(2)}, u32[]{:S(2)}) %all-to-all-start.1) | async-done | bytes 6291488 | tf_op jit(solution)/shard_map/all_to_all | solution.py:132
  109.3 9.2 %convolution_convert_fusion = bf16[12288,512]{1,0:T(8,128)(2,1)} fusion(bf16[12288,256]{1,0:T(8,128)(2,1)} %bitcast.16, bf16[256,512]{1,0:T(8,128)(2,1)S(1)} %copy-done.5), kind=kOutput, calls=%fused_computation.32 | convolution fusion | flops 3227516928 | bytes 19136512 | tf_op jit(solution)/shard_map/dot_general | solution.py:133
  118.4 299.1 %while.12 = (s32[]{:T(128)}, bf16[8,2,128,256]{3,2,1,0:T(8,128)(2,1)}, pred[8,2,4]{2,1,0:T(4,128)(4,1)S(1)}, bf16[8,2,128,256]{3,2,1,0:T(8,128)(2,1)S(1)}, s32[8...) while((s32[]{:T(128)}, bf16[8,2,128,256]{3,2,1,0:T(8,128)(2,1)}, ...), condition=%wide.region_6.7_spmd, body=%wide.region_3.6_spmd.sunk | while | flops 1088490496 | bytes 102069064 | solution.py:145
  118.5 5.2 %gather_fusion = bf16[8,128,512]{2,1,0:T(8,128)(2,1)S(1)} fusion(bf16[96,128,512]{2,1,0:T(8,128)(2,1)} %get-tuple-element.173, s32[1024]{0:T(1024)S(1)} %pad_clamp_fusion.3), kind=kCustom, calls=%fused_computation.clone.1 | custom fusion | bytes 2097184 | tf_op jit(solution)/shard_map/while/body/eval_jaxpr/gather | solution.py:141
  124.0 2.5 bitcast_multiply_fusion.5
  128.0 3.9 copy.56
  135.8 5.0 %div.99 = f32[2,128,4096]{2,1,0:T(8,128)} reshape(f32[2,128,8,512]{3,2,1,0:T(8,128)} %div.98) | data formatting | bytes 8388608 | tf_op jit(solution)/shard_map/while/body/eval_jaxpr/div | solution.py:35
  143.1 4.9 %sub.102 = f32[2,128,4096]{2,1,0:T(8,128)} reshape(f32[2,128,8,512]{3,2,1,0:T(8,128)} %sub.101) | data formatting | bytes 8388608 | tf_op jit(solution)/shard_map/while/body/eval_jaxpr/sub | solution.py:35
  148.1 7.8 %fusion.66 = bf16[8,2,128,256]{3,2,1,0:T(8,128)(2,1)} fusion(bf16[8,2,128,256]{3,2,1,0:T(8,128)(2,1)} %get-tuple-element.162, s32[]{:T(128)} %get-tuple-element.161, bf16[2,4096,256]{2,1,0:T(8,128)(2,1)} %get-tuple-element.152, f32[2,128,4096]{2,1,0:T(8,128)} %div.99, f32[2,128,4096]{2,1,0:T(8,128)} %sub.102, f32[2,128,4096]{2,1,0:T(8,128)} %copy-done.1, ...), kind=kOutput, calls=%fused_computation.14.clone.1 | convolution fusion | flops 541130752 | bytes 16916992 | tf_op jit(solution)/shard_map/while/body/eval_jaxpr/gyv,gvl->gyl/dot_general | solution.py:37
  155.9 5.2 %gather_fusion = bf16[8,128,512]{2,1,0:T(8,128)(2,1)S(1)} fusion(bf16[96,128,512]{2,1,0:T(8,128)(2,1)} %get-tuple-element.173, s32[1024]{0:T(1024)S(1)} %pad_clamp_fusion.3), kind=kCustom, calls=%fused_computation.clone.1 | custom fusion | bytes 2097184 | tf_op jit(solution)/shard_map/while/body/eval_jaxpr/gather | solution.py:141
  161.4 2.5 bitcast_multiply_fusion.5
  165.4 3.9 copy.56
  173.2 5.0 %div.99 = f32[2,128,4096]{2,1,0:T(8,128)} reshape(f32[2,128,8,512]{3,2,1,0:T(8,128)} %div.98) | data formatting | bytes 8388608 | tf_op jit(solution)/shard_map/while/body/eval_jaxpr/div | solution.py:35
  180.5 4.9 %sub.102 = f32[2,128,4096]{2,1,0:T(8,128)} reshape(f32[2,128,8,512]{3,2,1,0:T(8,128)} %sub.101) | data formatting | bytes 8388608 | tf_op jit(solution)/shard_map/while/body/eval_jaxpr/sub | solution.py:35
  185.5 7.8 %fusion.66 = bf16[8,2,128,256]{3,2,1,0:T(8,128)(2,1)} fusion(bf16[8,2,128,256]{3,2,1,0:T(8,128)(2,1)} %get-tuple-element.162, s32[]{:T(128)} %get-tuple-element.161, bf16[2,4096,256]{2,1,0:T(8,128)(2,1)} %get-tuple-element.152, f32[2,128,4096]{2,1,0:T(8,128)} %div.99, f32[2,128,4096]{2,1,0:T(8,128)} %sub.102, f32[2,128,4096]{2,1,0:T(8,128)} %copy-done.1, ...), kind=kOutput, calls=%fused_computation.14.clone.1 | convolution fusion | flops 541130752 | bytes 16916992 | tf_op jit(solution)/shard_map/while/body/eval_jaxpr/gyv,gvl->gyl/dot_general | solution.py:37
  193.3 5.2 %gather_fusion = bf16[8,128,512]{2,1,0:T(8,128)(2,1)S(1)} fusion(bf16[96,128,512]{2,1,0:T(8,128)(2,1)} %get-tuple-element.173, s32[1024]{0:T(1024)S(1)} %pad_clamp_fusion.3), kind=kCustom, calls=%fused_computation.clone.1 | custom fusion | bytes 2097184 | tf_op jit(solution)/shard_map/while/body/eval_jaxpr/gather | solution.py:141
  198.8 2.5 bitcast_multiply_fusion.5
  202.7 3.9 copy.56
  210.6 5.0 %div.99 = f32[2,128,4096]{2,1,0:T(8,128)} reshape(f32[2,128,8,512]{3,2,1,0:T(8,128)} %div.98) | data formatting | bytes 8388608 | tf_op jit(solution)/shard_map/while/body/eval_jaxpr/div | solution.py:35
  217.9 4.9 %sub.102 = f32[2,128,4096]{2,1,0:T(8,128)} reshape(f32[2,128,8,512]{3,2,1,0:T(8,128)} %sub.101) | data formatting | bytes 8388608 | tf_op jit(solution)/shard_map/while/body/eval_jaxpr/sub | solution.py:35
  222.9 7.8 %fusion.66 = bf16[8,2,128,256]{3,2,1,0:T(8,128)(2,1)} fusion(bf16[8,2,128,256]{3,2,1,0:T(8,128)(2,1)} %get-tuple-element.162, s32[]{:T(128)} %get-tuple-element.161, bf16[2,4096,256]{2,1,0:T(8,128)(2,1)} %get-tuple-element.152, f32[2,128,4096]{2,1,0:T(8,128)} %div.99, f32[2,128,4096]{2,1,0:T(8,128)} %sub.102, f32[2,128,4096]{2,1,0:T(8,128)} %copy-done.1, ...), kind=kOutput, calls=%fused_computation.14.clone.1 | convolution fusion | flops 541130752 | bytes 16916992 | tf_op jit(solution)/shard_map/while/body/eval_jaxpr/gyv,gvl->gyl/dot_general | solution.py:37
  230.7 5.2 %gather_fusion = bf16[8,128,512]{2,1,0:T(8,128)(2,1)S(1)} fusion(bf16[96,128,512]{2,1,0:T(8,128)(2,1)} %get-tuple-element.173, s32[1024]{0:T(1024)S(1)} %pad_clamp_fusion.3), kind=kCustom, calls=%fused_computation.clone.1 | custom fusion | bytes 2097184 | tf_op jit(solution)/shard_map/while/body/eval_jaxpr/gather | solution.py:141
  236.2 2.5 bitcast_multiply_fusion.5
  240.1 3.9 copy.56
  248.0 5.0 %div.99 = f32[2,128,4096]{2,1,0:T(8,128)} reshape(f32[2,128,8,512]{3,2,1,0:T(8,128)} %div.98) | data formatting | bytes 8388608 | tf_op jit(solution)/shard_map/while/body/eval_jaxpr/div | solution.py:35
  255.3 4.9 %sub.102 = f32[2,128,4096]{2,1,0:T(8,128)} reshape(f32[2,128,8,512]{3,2,1,0:T(8,128)} %sub.101) | data formatting | bytes 8388608 | tf_op jit(solution)/shard_map/while/body/eval_jaxpr/sub | solution.py:35
  260.2 7.8 %fusion.66 = bf16[8,2,128,256]{3,2,1,0:T(8,128)(2,1)} fusion(bf16[8,2,128,256]{3,2,1,0:T(8,128)(2,1)} %get-tuple-element.162, s32[]{:T(128)} %get-tuple-element.161, bf16[2,4096,256]{2,1,0:T(8,128)(2,1)} %get-tuple-element.152, f32[2,128,4096]{2,1,0:T(8,128)} %div.99, f32[2,128,4096]{2,1,0:T(8,128)} %sub.102, f32[2,128,4096]{2,1,0:T(8,128)} %copy-done.1, ...), kind=kOutput, calls=%fused_computation.14.clone.1 | convolution fusion | flops 541130752 | bytes 16916992 | tf_op jit(solution)/shard_map/while/body/eval_jaxpr/gyv,gvl->gyl/dot_general | solution.py:37
  268.1 5.2 %gather_fusion = bf16[8,128,512]{2,1,0:T(8,128)(2,1)S(1)} fusion(bf16[96,128,512]{2,1,0:T(8,128)(2,1)} %get-tuple-element.173, s32[1024]{0:T(1024)S(1)} %pad_clamp_fusion.3), kind=kCustom, calls=%fused_computation.clone.1 | custom fusion | bytes 2097184 | tf_op jit(solution)/shard_map/while/body/eval_jaxpr/gather | solution.py:141
  277.5 3.9 copy.56
  285.4 5.0 %div.99 = f32[2,128,4096]{2,1,0:T(8,128)} reshape(f32[2,128,8,512]{3,2,1,0:T(8,128)} %div.98) | data formatting | bytes 8388608 | tf_op jit(solution)/shard_map/while/body/eval_jaxpr/div | solution.py:35
  292.6 4.9 %sub.102 = f32[2,128,4096]{2,1,0:T(8,128)} reshape(f32[2,128,8,512]{3,2,1,0:T(8,128)} %sub.101) | data formatting | bytes 8388608 | tf_op jit(solution)/shard_map/while/body/eval_jaxpr/sub | solution.py:35
  297.6 7.8 %fusion.66 = bf16[8,2,128,256]{3,2,1,0:T(8,128)(2,1)} fusion(bf16[8,2,128,256]{3,2,1,0:T(8,128)(2,1)} %get-tuple-element.162, s32[]{:T(128)} %get-tuple-element.161, bf16[2,4096,256]{2,1,0:T(8,128)(2,1)} %get-tuple-element.152, f32[2,128,4096]{2,1,0:T(8,128)} %div.99, f32[2,128,4096]{2,1,0:T(8,128)} %sub.102, f32[2,128,4096]{2,1,0:T(8,128)} %copy-done.1, ...), kind=kOutput, calls=%fused_computation.14.clone.1 | convolution fusion | flops 541130752 | bytes 16916992 | tf_op jit(solution)/shard_map/while/body/eval_jaxpr/gyv,gvl->gyl/dot_general | solution.py:37
  305.5 5.2 %gather_fusion = bf16[8,128,512]{2,1,0:T(8,128)(2,1)S(1)} fusion(bf16[96,128,512]{2,1,0:T(8,128)(2,1)} %get-tuple-element.173, s32[1024]{0:T(1024)S(1)} %pad_clamp_fusion.3), kind=kCustom, calls=%fused_computation.clone.1 | custom fusion | bytes 2097184 | tf_op jit(solution)/shard_map/while/body/eval_jaxpr/gather | solution.py:141
  310.9 2.5 bitcast_multiply_fusion.5
  314.9 3.9 copy.56
  322.8 5.0 %div.99 = f32[2,128,4096]{2,1,0:T(8,128)} reshape(f32[2,128,8,512]{3,2,1,0:T(8,128)} %div.98) | data formatting | bytes 8388608 | tf_op jit(solution)/shard_map/while/body/eval_jaxpr/div | solution.py:35
  330.0 4.9 %sub.102 = f32[2,128,4096]{2,1,0:T(8,128)} reshape(f32[2,128,8,512]{3,2,1,0:T(8,128)} %sub.101) | data formatting | bytes 8388608 | tf_op jit(solution)/shard_map/while/body/eval_jaxpr/sub | solution.py:35
  335.0 7.8 %fusion.66 = bf16[8,2,128,256]{3,2,1,0:T(8,128)(2,1)} fusion(bf16[8,2,128,256]{3,2,1,0:T(8,128)(2,1)} %get-tuple-element.162, s32[]{:T(128)} %get-tuple-element.161, bf16[2,4096,256]{2,1,0:T(8,128)(2,1)} %get-tuple-element.152, f32[2,128,4096]{2,1,0:T(8,128)} %div.99, f32[2,128,4096]{2,1,0:T(8,128)} %sub.102, f32[2,128,4096]{2,1,0:T(8,128)} %copy-done.1, ...), kind=kOutput, calls=%fused_computation.14.clone.1 | convolution fusion | flops 541130752 | bytes 16916992 | tf_op jit(solution)/shard_map/while/body/eval_jaxpr/gyv,gvl->gyl/dot_general | solution.py:37
  342.9 5.2 %gather_fusion = bf16[8,128,512]{2,1,0:T(8,128)(2,1)S(1)} fusion(bf16[96,128,512]{2,1,0:T(8,128)(2,1)} %get-tuple-element.173, s32[1024]{0:T(1024)S(1)} %pad_clamp_fusion.3), kind=kCustom, calls=%fused_computation.clone.1 | custom fusion | bytes 2097184 | tf_op jit(solution)/shard_map/while/body/eval_jaxpr/gather | solution.py:141
  348.3 2.5 bitcast_multiply_fusion.5
  352.3 3.9 copy.56
  360.2 5.0 %div.99 = f32[2,128,4096]{2,1,0:T(8,128)} reshape(f32[2,128,8,512]{3,2,1,0:T(8,128)} %div.98) | data formatting | bytes 8388608 | tf_op jit(solution)/shard_map/while/body/eval_jaxpr/div | solution.py:35
  367.4 4.9 %sub.102 = f32[2,128,4096]{2,1,0:T(8,128)} reshape(f32[2,128,8,512]{3,2,1,0:T(8,128)} %sub.101) | data formatting | bytes 8388608 | tf_op jit(solution)/shard_map/while/body/eval_jaxpr/sub | solution.py:35
  372.4 7.8 %fusion.66 = bf16[8,2,128,256]{3,2,1,0:T(8,128)(2,1)} fusion(bf16[8,2,128,256]{3,2,1,0:T(8,128)(2,1)} %get-tuple-element.162, s32[]{:T(128)} %get-tuple-element.161, bf16[2,4096,256]{2,1,0:T(8,128)(2,1)} %get-tuple-element.152, f32[2,128,4096]{2,1,0:T(8,128)} %div.99, f32[2,128,4096]{2,1,0:T(8,128)} %sub.102, f32[2,128,4096]{2,1,0:T(8,128)} %copy-done.1, ...), kind=kOutput, calls=%fused_computation.14.clone.1 | convolution fusion | flops 541130752 | bytes 16916992 | tf_op jit(solution)/shard_map/while/body/eval_jaxpr/gyv,gvl->gyl/dot_general | solution.py:37
  380.3 5.2 %gather_fusion = bf16[8,128,512]{2,1,0:T(8,128)(2,1)S(1)} fusion(bf16[96,128,512]{2,1,0:T(8,128)(2,1)} %get-tuple-element.173, s32[1024]{0:T(1024)S(1)} %pad_clamp_fusion.3), kind=kCustom, calls=%fused_computation.clone.1 | custom fusion | bytes 2097184 | tf_op jit(solution)/shard_map/while/body/eval_jaxpr/gather | solution.py:141
  385.7 2.5 bitcast_multiply_fusion.5
  389.7 3.9 copy.56
  397.6 5.0 %div.99 = f32[2,128,4096]{2,1,0:T(8,128)} reshape(f32[2,128,8,512]{3,2,1,0:T(8,128)} %div.98) | data formatting | bytes 8388608 | tf_op jit(solution)/shard_map/while/body/eval_jaxpr/div | solution.py:35
  404.8 4.9 %sub.102 = f32[2,128,4096]{2,1,0:T(8,128)} reshape(f32[2,128,8,512]{3,2,1,0:T(8,128)} %sub.101) | data formatting | bytes 8388608 | tf_op jit(solution)/shard_map/while/body/eval_jaxpr/sub | solution.py:35
  409.8 7.8 %fusion.66 = bf16[8,2,128,256]{3,2,1,0:T(8,128)(2,1)} fusion(bf16[8,2,128,256]{3,2,1,0:T(8,128)(2,1)} %get-tuple-element.162, s32[]{:T(128)} %get-tuple-element.161, bf16[2,4096,256]{2,1,0:T(8,128)(2,1)} %get-tuple-element.152, f32[2,128,4096]{2,1,0:T(8,128)} %div.99, f32[2,128,4096]{2,1,0:T(8,128)} %sub.102, f32[2,128,4096]{2,1,0:T(8,128)} %copy-done.1, ...), kind=kOutput, calls=%fused_computation.14.clone.1 | convolution fusion | flops 541130752 | bytes 16916992 | tf_op jit(solution)/shard_map/while/body/eval_jaxpr/gyv,gvl->gyl/dot_general | solution.py:37
  420.3 4.6 all-to-all-start.2
  427.4 8.3 %all-to-all-done.2 = bf16[8,4,64,256]{3,2,0,1:T(8,128)(2,1)S(1)} async-done(((bf16[8,4,64,256]{3,2,0,1:T(8,128)(2,1)}), bf16[8,4,64,256]{3,2,0,1:T(8,128)(2,1)S(1)}, u32[]{:S(2)}, u32[]{:S(2)}) %all-to-all-start.2) | async-done | bytes 1048608 | tf_op jit(solution)/shard_map/all_to_all | solution.py:157
  439.8 6.8 %bitcast_multiply_fusion.3 = (bf16[64,256,256]{2,1,0:T(8,128)(2,1)}, bf16[64,256,256]{2,1,0:T(8,128)(2,1)}) fusion(bf16[256,256]{1,0:T(8,128)(2,1)S(1)} %bitcast.162, bf16[64,32,256]{2,1,0:T(8,128)(2,1)S(1)} %get-tuple-element.102, bf16[64,32,256]{2,1,0:T(8,128)(2,1)S(1)} %get-tuple-element.103), kind=kLoop, calls=%fused_computation.34 | loop fusion | flops 8388608 | bytes 19005440 | tf_op jit(solution)/shard_map/mul | solution.py:18
  446.6 6.3 %convolution_multiply_fusion.1 = f32[64,32,256]{2,1,0:T(8,128)S(1)} fusion(bf16[64,256,256]{2,1,0:T(8,128)(2,1)} %get-tuple-element.104, bf16[64,32,768]{2,1,0:T(8,128)(2,1)} %copy-done.4), kind=kOutput, calls=%fused_computation.53 | convolution fusion | flops 268959744 | bytes 11534336 | tf_op jit(solution)/shard_map/csd,cxd->csx/dot_general | solution.py:59
  452.9 2.8 copy.38
  455.7 3.2 select_reduce_fusion
  461.1 4.2 copy.39
  465.3 5.1 %fusion.11 = f32[64,32,8,32]{0,3,2,1:T(8,128)} fusion(f32[64,32,8,32]{0,3,2,1:T(8,128)} %bitcast.150, f32[64,32,8]{0,2,1:T(8,128)S(1)} %select_reduce_fusion, pred[64,32,32]{0,2,1:T(8,128)(4,1)S(1)} %and_or_fusion), kind=kOutput, calls=%fused_computation.31 | output fusion | flops 1064991 | bytes 4325376 | tf_op jit(solution)/shard_map/div | solution.py:70
  470.4 4.2 copy.40
  474.6 9.5 %fusion.16 = f32[32,1,1,64,256]{4,0,3,2,1:T(8,128)} fusion(f32[4,8,1,64,256]{4,3,1,0,2:T(8,128)} %copy-done.3, bf16[64,256,256]{2,1,0:T(8,128)(2,1)} %get-tuple-element.105, f32[64,32,256]{2,1,0:T(8,128)} %copy.40, f32[64,32,256]{2,1,0:T(8,128)} %copy.39, pred[64,32,256]{2,1,0:T(32,128)(4,1)S(1)} %copy.37, ...), kind=kOutput, calls=%fused_computation.46 | convolution fusion | flops 540016640 | bytes 19529728 | tf_op jit(solution)/shard_map/csf,fz->csz/dot_general | solution.py:75
  484.1 4.1 copy.41
  (219 shorter events, 84.7 us)
Async XLA Ops:
  0.0 436.0 %copy-start = (bf16[256,768]{1,0:T(8,128)(2,1)S(1)}, bf16[256,768]{1,0:T(8,128)(2,1)}, u32[]{:S(2)}) copy-start(bf16[256,768]{1,0:T(8,128)(2,1)} %param.20) | copy-start | bytes 1179652
  26.3 5.2 %copy-start.9 = (bf16[32,256]{1,0:T(8,128)(2,1)S(1)}, bf16[32,256]{1,0:T(8,128)(2,1)}, u32[]{:S(2)}) copy-start(bf16[32,256]{1,0:T(8,128)(2,1)} %param.19) | copy-start | bytes 49156
  26.3 5.8 %copy-start.13 = (s32[256]{0:T(256)S(1)}, s32[256]{0:T(256)}, u32[]{:S(2)}) copy-start(s32[256]{0:T(256)} %param.15) | copy-start | bytes 3076
  26.3 7.1 %copy-start.2 = (bf16[8,256,256]{2,1,0:T(8,128)(2,1)S(1)}, bf16[8,256,256]{2,1,0:T(8,128)(2,1)}, u32[]{:S(2)}) copy-start(bf16[8,256,256]{2,1,0:T(8,128)(2,1)} %param.12) | copy-start | bytes 3145732
  26.3 7.1 %copy-start.8 = (bf16[256,256]{1,0:T(8,128)(2,1)S(1)}, bf16[256,256]{1,0:T(8,128)(2,1)}, u32[]{:S(2)}) copy-start(bf16[256,256]{1,0:T(8,128)(2,1)} %param.16) | copy-start | bytes 393220
  26.3 83.0 %copy-start.5 = (bf16[256,512]{1,0:T(8,128)(2,1)S(1)}, bf16[256,512]{1,0:T(8,128)(2,1)}, u32[]{:S(2)}) copy-start(bf16[256,512]{1,0:T(8,128)(2,1)} %param.17) | copy-start | bytes 786436
  26.3 83.0 %all-to-all-start.1 = ((bf16[32,3,128,256]{3,2,1,0:T(8,128)(2,1)}), bf16[32,3,128,256]{3,2,1,0:T(8,128)(2,1)}, u32[]{:S(2)}, u32[]{:S(2)}) async-start(bf16[32,3,128,256]{3,2,1,0:T(8,128)(2,1)} %bitcast.152), calls=%async_computation.1 | async-start | bytes 12582912 | tf_op jit(solution)/shard_map/all_to_all | solution.py:132
  128.0 3.9 copy-start.1
  165.3 3.9 copy-start.1
  202.7 3.9 copy-start.1
  240.1 3.9 copy-start.1
  277.5 3.9 copy-start.1
  314.9 3.9 copy-start.1
  352.3 3.9 copy-start.1
  389.7 3.9 copy-start.1
  417.6 7.3 %copy-start.12 = (s32[64]{0:T(128)S(1)}, s32[64]{0:T(128)}, u32[]{:S(2)}) copy-start(s32[64]{0:T(128)} %dynamic_slice.24) | copy-start | bytes 772
  417.6 7.3 %copy-start.10 = (pred[32,32]{1,0:T(8,128)(4,1)S(1)}, pred[32,32]{1,0:T(8,128)(4,1)}, u32[]{:S(2)}) copy-start(pred[32,32]{1,0:T(8,128)(4,1)} %get-tuple-element.107) | copy-start | bytes 3076
  417.6 7.3 %copy-start.11 = (pred[32,32]{1,0:T(8,128)(4,1)S(1)}, pred[32,32]{1,0:T(8,128)(4,1)}, u32[]{:S(2)}) copy-start(pred[32,32]{1,0:T(8,128)(4,1)} %get-tuple-element.108) | copy-start | bytes 3076
  420.3 15.7 %copy-start.7 = (f32[32,256]{1,0:T(8,128)S(1)}, f32[32,256]{1,0:T(8,128)}, u32[]{:S(2)}) copy-start(f32[32,256]{1,0:T(8,128)} %convert_element_type.95) | copy-start | bytes 98308
  420.3 15.5 %all-to-all-start.2 = ((bf16[8,4,64,256]{3,2,0,1:T(8,128)(2,1)}), bf16[8,4,64,256]{3,2,0,1:T(8,128)(2,1)S(1)}, u32[]{:S(2)}, u32[]{:S(2)}) async-start(bf16[8,4,64,256]{3,2,0,1:T(8,128)(2,1)} %copy.35), calls=%async_computation.2 | async-start | bytes 2097152 | tf_op jit(solution)/shard_map/all_to_all | solution.py:157
  436.0 2.4 copy-start.3
  438.2 1.7 copy-start.4
  470.4 4.3 copy-start.6
where the time goes:
time: 492 us; the launch traced here: 488 us
  local copies, waits for them, and re-layouts  225 us (46%)
  matrix products  103 us (21%)
  waiting for transfers between devices  83.8 us (17%)
  other arithmetic  50 us (10%)
  blocking collectives  15.4 us (3%)
  starting transfers between devices  9.63 us (2%)
    all_to_all x1, waiting for transfers between devices, local(): lax.all_to_all(outgoing, 'vert', split_axis=0, concat_axis=0, tiled=True)  75.4 us
    dot_general x8, matrix products, attend_tiles(): jnp.einsum('gyv,gvl->gyl', weight_matrices, widened_values, preferred_ele...  62.1 us
    div x16, local copies, waits for them, and re-layouts, attend_tiles(): jax.nn.softmax(scores, axis=-1).astype(jnp.bfloat16)  58.1 us
    sub x16, local copies, waits for them, and re-layouts, attend_tiles(): jax.nn.softmax(scores, axis=-1).astype(jnp.bfloat16)  57.8 us
    gather x8, local copies, waits for them, and re-layouts, per_snapshot(): fetched[slot_block].reshape(blocks, tile_slots * TILE, 2 * model_width)  41.5 us
    while x56, local copies, waits for them, and re-layouts  31.9 us
    mul x9, other arithmetic, widen_heads(): spread = rows[:, None, :, :] * column_mask[None, :, None, :]  26.5 us
    all_to_all x1, blocking collectives, local(): lax.all_to_all(outgoing_codes.reshape(peer_count, capacity), 'vert', spli...  15.4 us
  transfers between devices with their start and end apart: 2, of which 2 were waited for; matrix products, arithmetic and copies ran while one was open for 1% of the time, Pallas kernels for 0%

commit v1 on v0

v1 whole, which is shorter than its diff:
```python
import functools

import jax
import jax.numpy as jnp
from jax import lax
from jax.experimental import pallas as pl
from jax.experimental.pallas import tpu as pltpu
from jax.sharding import PartitionSpec as P

HEADS = 8
TILE = 128
D = 256
HS = D // HEADS
KT = 4
BLOCKS = 16
RING = 4
RANKS = 3
SLOTS = 2 * RING * RING * RANKS
SCALE = 1.4426950408889634 * HS**-0.5
MESH = pl.DeviceIdType.MESH
NT = (((1,), (1,)), ((), ()))
TN = (((0,), (0,)), ((), ()))
NN = (((1,), (0,)), ((), ()))
ORDER = (0, 1, 3, 2)


def dot(a, b, dims=NN):
    return lax.dot_general(a, b, dims, preferred_element_type=jnp.float32)


def vert_id(z, x, core):
    return (z * RING + x) * 2 + core


def position():
    v = lax.axis_index("vert")
    return v // (2 * RING), (v // 2) % RING, v % 2


def prep_kernel(cols, counts, req, blk, table, used):
    z, x, core = position()

    @pl.loop(0, SLOTS)
    def _(n):
        blk[n] = 0

    @pl.loop(0, 8)
    def _(row):
        for n in range(RING * RANKS):
            req[row, n] = 0
        for n in range(RING):
            used[row, n] = 0

    @pl.loop(0, BLOCKS)
    def _(b):
        live = counts[b]
        for k in range(KT):
            col = cols[b, k]
            alive = k < live
            owner = jnp.where(alive, col // 2, 0)
            oz, ox, oc = owner // (2 * RING), (owner // 2) % RING, owner % 2
            dz, dx = (oz - z + RING) % RING, (x - ox + RING) % RING
            ez, ex = (z - oz + RING) % RING, (ox - x + RING) % RING
            i = jnp.where(oc == 0, dx, ez)
            j = jnp.where(oc == 0, dz, ex)
            row = jnp.where(oc == core, 0, RING) + i
            rank = used[row, j]
            place = (row * RING + j) * RANKS + rank

            @pl.when(alive)
            def _():
                used[row, j] = rank + 1
                req[row, j * RANKS + rank] = (b // 2) * 2 + col % 2
                blk[place] = b

            table[b, k] = jnp.where(alive, place, -1)


def fetch_kernel(
    req, blk, table, wire, feat, wq_in, wkv_in, wso, arr,
    codes_v, codes, ag1, ag2, ag3, stage, recv, wq, wt, part, top, total, hid,
    req_send, req_recv, loc_sem, ag_send, ag_recv, tile_send, tile_recv, snap_send, snap_recv, own_sem,
):
    z, x, core = position()
    y = lax.axis_index("snap")
    flat = core == 0

    def gather_peer(j):
        return vert_id(
            jnp.where(flat, (z + j) % RING, z), jnp.where(flat, x, (x + j) % RING), core
        )

    def dest(row):
        i = row % RING
        other = row // RING
        return vert_id(
            jnp.where(flat, z, (z + i) % RING),
            jnp.where(flat, (x + i) % RING, x),
            (core + other) % 2,
        )

    def relay(row):
        i = row % RING
        c = (core + row // RING) % 2
        return vert_id(
            jnp.where(c == 0, z, (z + RING - i) % RING),
            jnp.where(c == 0, (x + RING - i) % RING, x),
            c,
        )

    barrier = pltpu.get_barrier_semaphore()
    greet = [gather_peer(1), gather_peer(2), gather_peer(3)]
    greet += [dest(r) for r in range(1, 8)]
    greet += [relay(r) for r in range(5, 8)]
    for v in greet:
        pl.semaphore_signal(barrier, inc=1, device_id=(y, v), device_id_type=MESH)
    for i in range(1, RING):
        pl.semaphore_signal(
            barrier, inc=1, device_id=((y + i) % RING, lax.axis_index("vert")), device_id_type=MESH
        )
    pl.semaphore_wait(barrier, len(greet) + RING - 1)

    def ask(row):
        return pltpu.make_async_remote_copy(
            src_ref=wire.at[row],
            dst_ref=codes_v.at[row],
            send_sem=req_send.at[row],
            recv_sem=req_recv.at[row],
            device_id=(y, relay(row)),
            device_id_type=MESH,
        )

    for row in range(1, 8):
        ask(row).start()

    gathered = {1: ag1, 2: ag2, 3: ag3}

    def share(j):
        return pltpu.make_async_remote_copy(
            src_ref=feat,
            dst_ref=gathered[j],
            send_sem=ag_send.at[j - 1],
            recv_sem=ag_recv.at[j - 1],
            device_id=(y, gather_peer(RING - j)),
            device_id_type=MESH,
        )

    for j in ORDER[1:]:
        share(j).start()

    wt[0] = wq_in[...].astype(jnp.float32).T.astype(jnp.bfloat16)
    wt[1] = wkv_in[:, D:].astype(jnp.float32).T.astype(jnp.bfloat16)

    @pl.loop(0, BLOCKS)
    def _(b):
        q = (dot(wt[0], feat[b], NT) * SCALE).astype(jnp.bfloat16)
        zero = jnp.zeros((HS, TILE), jnp.bfloat16)
        for h in range(HEADS):
            p, lo = h // 2, (h % 2) * TILE
            base = (h % 4) * HS
            for g in range(4):
                if g != h % 4:
                    wq[b, p, g * HS : (g + 1) * HS, lo : lo + TILE] = zero
            wq[b, p, base : base + HS, lo : lo + TILE] = q[h * HS : (h + 1) * HS]

    for row in range(1, 8):
        ask(row).wait()
    down = pltpu.make_async_copy(codes_v.at[pl.ds(1, 7)], codes.at[pl.ds(1, 7)], loc_sem)
    down.start()
    down.wait()

    def send(row, j):
        return pltpu.make_async_remote_copy(
            src_ref=stage.at[row, j],
            dst_ref=recv.at[row, j],
            send_sem=tile_send.at[row, j],
            recv_sem=tile_recv.at[row, j],
            device_id=(y, dest(row)),
            device_id_type=MESH,
        )

    for j in ORDER:
        if j:
            share(j).wait_recv()
        source = gathered[j] if j else feat

        @pl.loop(1, 8)
        def _(row):
            for r in range(RANKS):
                stage[row, j, r] = source[codes[row, 0, j * RANKS + r]]
            send(row, j).start()

        for r in range(RANKS):
            recv[0, j, r] = source[req[0, j * RANKS + r]]

    def attend(row, j, r):
        n = (row * RING + j) * RANKS + r
        b = blk[n]
        rows = recv[row, j, r]
        keys = dot(rows, wkv_in[:, :D]).astype(jnp.bfloat16)
        values = dot(wt[1], rows, NT).astype(jnp.bfloat16)
        for p in range(HEADS // 2):
            half = (p // 2) * TILE
            s = dot(keys[:, half : half + TILE], wq[b, p])
            m = jnp.max(s, axis=0, keepdims=True)
            e = jnp.exp2(s - m)
            t = jnp.sum(e, axis=0, keepdims=True)
            o = dot(values[2 * p * HS : 2 * (p + 1) * HS], e.astype(jnp.bfloat16))
            for g in range(2):
                h = 2 * p + g
                top[n, h : h + 1] = m[:, g * TILE : (g + 1) * TILE]
                total[n, h : h + 1] = t[:, g * TILE : (g + 1) * TILE]
                part[n, h * HS : (h + 1) * HS] = o[g * HS : (g + 1) * HS, g * TILE : (g + 1) * TILE]

    for j in ORDER:
        for r in range(RANKS):
            attend(0, j, r)

        @pl.loop(1, 8)
        def _(row):
            send(row, j).wait_recv()

            @pl.loop(0, RANKS)
            def _(r):
                attend(row, j, r)

    def spread(i, half):
        group = (y + i) % RING
        return pltpu.make_async_remote_copy(
            src_ref=hid.at[pl.ds(half * 4, 4), pl.ds(group * 64, 64)],
            dst_ref=arr.at[pl.ds(y * 8 + half * 4, 4)],
            send_sem=snap_send.at[half, i],
            recv_sem=snap_recv.at[half, i],
            device_id=(group, lax.axis_index("vert")),
            device_id_type=MESH,
        )

    for half in range(2):

        @pl.loop(half * 4, half * 4 + 4)
        def _(s):
            for u in range(2):
                b = s * 2 + u
                slots, live, tops = [], [], []
                for k in range(KT):
                    slot = table[b, k]
                    alive = slot >= 0
                    slot = jnp.where(alive, slot, 0)
                    slots.append(slot)
                    live.append(jnp.where(alive, jnp.float32(0), jnp.float32(-jnp.inf)))
                    tops.append(top[slot] + live[k])
                m = functools.reduce(jnp.maximum, tops)
                weights = [jnp.exp2(t - m) for t in tops]
                denominator = sum(weights[k] * total[slots[k]] for k in range(KT))
                weights = [w / denominator for w in weights]
                parts = []
                for h in range(HEADS):
                    parts.append(
                        sum(
                            weights[k][h : h + 1] * part[slots[k], h * HS : (h + 1) * HS]
                            for k in range(KT)
                        )
                    )
                attended = jnp.concatenate(parts, axis=0).T.astype(jnp.bfloat16)
                update = dot(attended, wso[...])
                hid[s, u * TILE : (u + 1) * TILE] = (feat[b].astype(jnp.float32) + update).astype(
                    jnp.bfloat16
                )

        for i in (2, 1, 3):
            spread(i, half).start()

    own = pltpu.make_async_copy(hid.at[:, pl.ds(y * 64, 64)], arr.at[pl.ds(y * 8, 8)], own_sem)
    own.start()
    own.wait()
    for half in range(2):
        for i in range(1, RING):
            spread(i, half).wait()
    for j in ORDER:
        if j:
            share(j).wait_send()

        @pl.loop(1, 8)
        def _(row):
            send(row, j).wait_send()


def time_kernel(births, arr, pos, wqkv, wo, out, wt):
    y = lax.axis_index("snap")
    step = pl.program_id(0)

    @pl.when(step == 0)
    def _():
        wt[0] = wqkv[:, :D].astype(jnp.float32).T.astype(jnp.bfloat16)
        wt[1] = wqkv[:, 2 * D :].astype(jnp.float32).T.astype(jnp.bfloat16)

    snaps = pos.shape[0]
    n = snaps * 8
    hidden = arr[...].astype(jnp.float32)
    positions = pos[...].astype(jnp.float32)[:, None, :]
    lane_head = lax.broadcasted_iota(jnp.int32, (1, TILE), 1) // HS
    vertex = lax.broadcasted_iota(jnp.int32, (1, 8, 1), 1)
    lane = lax.broadcasted_iota(jnp.int32, (1, 1, n), 2)
    key_snap = lax.broadcasted_iota(jnp.int32, (snaps, 1, 1), 0)
    for g in range(2):
        base = y * 64 + step * 16 + g * 8
        birth = jnp.zeros((1, 8, 1), jnp.int32)
        for v in range(8):
            birth = jnp.where(vertex == v, births[base + v], birth)
        query_snap = lane // 8
        allowed = (lane % 8 == vertex) & (
            (query_snap == key_snap) | ((query_snap >= key_snap) & (key_snap >= birth))
        )
        bias = jnp.where(allowed, jnp.float32(0), jnp.float32(-jnp.inf)).reshape(n, n)
        mine = hidden[:, g * 8 : (g + 1) * 8]
        rows = (mine + positions).reshape(n, D).astype(jnp.bfloat16)
        q = (dot(wt[0], rows, NT) * SCALE).astype(jnp.bfloat16)
        keys = dot(rows, wqkv[:, D : 2 * D]).astype(jnp.bfloat16)
        values = dot(wt[1], rows, NT).astype(jnp.bfloat16)
        mixed = []
        for h in range(HEADS):
            half = (h // 4) * TILE
            mask = (lane_head == h % 4).astype(jnp.float32).astype(jnp.bfloat16)
            s = dot(keys[:, half : half + TILE] * mask, q[half : half + TILE]) + bias
            m = jnp.max(s, axis=0, keepdims=True)
            e = jnp.exp2(s - m)
            t = jnp.sum(e, axis=0, keepdims=True)
            o = dot(values[h * HS : (h + 1) * HS], e.astype(jnp.bfloat16))
            mixed.append(o / t)
        mixed = jnp.concatenate(mixed, axis=0).T.astype(jnp.bfloat16)
        out[:, g * 8 : (g + 1) * 8] = mine + dot(mixed, wo[...]).reshape(snaps, 8, D)


def local(features, tile_cols, counts, births, wq, wkv, wso, pos, wqkv, wo):
    snaps, rows, width = features.shape
    smem = pl.BlockSpec(memory_space=pltpu.SMEM)
    vmem = pl.BlockSpec(memory_space=pltpu.VMEM)
    hbm = pl.BlockSpec(memory_space=pl.ANY)
    dma = pltpu.SemaphoreType.DMA
    req, blk, table = pl.pallas_call(
        prep_kernel,
        out_shape=(
            jax.ShapeDtypeStruct((8, 128), jnp.int32),
            jax.ShapeDtypeStruct((SLOTS,), jnp.int32),
            jax.ShapeDtypeStruct((BLOCKS, KT), jnp.int32),
        ),
        in_specs=[smem] * 2,
        out_specs=(smem,) * 3,
        scratch_shapes=[pltpu.SMEM((8, RING), jnp.int32)],
        name="rank_entries",
    )(tile_cols.reshape(BLOCKS, KT), counts.reshape(BLOCKS))
    half = jnp.bfloat16
    arrived = pl.pallas_call(
        fetch_kernel,
        out_shape=jax.ShapeDtypeStruct((RING * snaps, rows // RING, width), half),
        in_specs=[smem] * 3 + [vmem] * 5,
        out_specs=hbm,
        scratch_shapes=[
            pltpu.VMEM((8, 1, 128), jnp.int32),
            pltpu.SMEM((8, 1, 128), jnp.int32),
            pltpu.VMEM((BLOCKS, TILE, width), half),
            pltpu.VMEM((BLOCKS, TILE, width), half),
            pltpu.VMEM((BLOCKS, TILE, width), half),
            pltpu.VMEM((8, RING, RANKS, TILE, width), half),
            pltpu.VMEM((8, RING, RANKS, TILE, width), half),
            pltpu.VMEM((BLOCKS, HEADS // 2, TILE, 2 * TILE), half),
            pltpu.VMEM((2, width, width), half),
            pltpu.VMEM((SLOTS, width, TILE), jnp.float32),
            pltpu.VMEM((SLOTS, HEADS, TILE), jnp.float32),
            pltpu.VMEM((SLOTS, HEADS, TILE), jnp.float32),
            pltpu.VMEM((snaps, rows, width), half),
            dma((8,)), dma((8,)), dma, dma((3,)), dma((3,)),
            dma((8, RING)), dma((8, RING)), dma((2, RING)), dma((2, RING)), dma,
        ],
        compiler_params=pltpu.CompilerParams(
            collective_id=0, has_side_effects=True, vmem_limit_bytes=56 * 2**20
        ),
        name="fetch_attend",
    )(req, blk, table, req.reshape(8, 1, 128), features.reshape(BLOCKS, TILE, width), wq, wkv, wso)
    count = rows // RING
    result = pl.pallas_call(
        time_kernel,
        out_shape=jax.ShapeDtypeStruct((RING * snaps, count, width), jnp.float32),
        grid=(count // 16,),
        in_specs=[
            smem,
            pl.BlockSpec((RING * snaps, 16, width), lambda i: (0, i, 0)),
            pl.BlockSpec(pos.shape, lambda i: (0, 0)),
            pl.BlockSpec(wqkv.shape, lambda i: (0, 0)),
            pl.BlockSpec(wo.shape, lambda i: (0, 0)),
        ],
        out_specs=pl.BlockSpec((RING * snaps, 16, width), lambda i: (0, i, 0)),
        scratch_shapes=[pltpu.VMEM((2, width, width), half)],
        compiler_params=pltpu.CompilerParams(vmem_limit_bytes=48 * 2**20),
        name="attend_time",
    )(births, arrived, pos, wqkv, wo)
    return result[:, None, None]


def solution(mesh):
    placed = (
        P("snap", "vert", None), P("snap", "vert", None), P("snap", "vert"), P("vert"),
        P(), P(), P(), P(), P(), P(),
    )
    return jax.shard_map(
        local,
        mesh=mesh,
        in_specs=placed,
        out_specs=P(None, "vert", "snap", None, None),
        check_vma=False,
    )
```

time: 492 us -> 185 us (0.38)
  local copies, waits for them, and re-layouts: 225 us -> 3.99 us
  Pallas kernels: 0 us -> 181 us
  matrix products: 103 us -> 0 us
  waiting for transfers between devices: 83.8 us -> 0 us
  other arithmetic: 50 us -> 0 us
  blocking collectives: 15.4 us -> 0 us
  starting transfers between devices: 9.63 us -> 0 us
    pallas_call x0 -> x3, Pallas kernels: none -> 181 us  [the longest x1 154 us: local(): pl.pallas_call(fetch_kernel, out_shape=jax.ShapeDtypeStruct((RING * snaps...]
    dot_general x22 -> x0, matrix products: 103 us -> none  [the longest x8 62.1 us: attend_tiles(): jnp.einsum('gyv,gvl->gyl', weight_matrices, widened_values, preferred_ele...]
    all_to_all x2 -> x0, waiting for transfers between devices: 83.8 us -> none  [the longest x1 75.4 us: local(): lax.all_to_all(outgoing, 'vert', split_axis=0, concat_axis=0, tiled=True)]
    sub x18 -> x0, local copies, waits for them, and re-layouts: 64.3 us -> none  [the longest x16 57.8 us: attend_tiles(): jax.nn.softmax(scores, axis=-1).astype(jnp.bfloat16)]
    div x17 -> x0, local copies, waits for them, and re-layouts: 62.3 us -> none  [the longest x16 58.1 us: attend_tiles(): jax.nn.softmax(scores, axis=-1).astype(jnp.bfloat16)]
    gather x9 -> x0, local copies, waits for them, and re-layouts: 48.7 us -> none  [the longest x8 41.5 us: per_snapshot(): fetched[slot_block].reshape(blocks, tile_slots * TILE, 2 * model_width)]
    while x56 -> x0, local copies, waits for them, and re-layouts: 31.9 us -> none
    mul x11 -> x0, other arithmetic: 26.6 us -> none  [the longest x9 26.5 us: widen_heads(): spread = rows[:, None, :, :] * column_mask[None, :, None, :]]
  transfers between devices with their start and end apart: 2 -> 0, of which waited for: 2 -> 0; matrix products, arithmetic and copies ran while one was open for 1% -> 0% of each run, Pallas kernels for 0% -> 0%
where the time goes in v1:
time: 185 us
  Pallas kernels  181 us (98%)
  local copies, waits for them, and re-layouts  3.99 us (2%)
    pallas_call x1, Pallas kernels, local(): pl.pallas_call(fetch_kernel, out_shape=jax.ShapeDtypeStruct((RING * snaps...  154 us
    pallas_call x1, Pallas kernels, local(): pl.pallas_call(time_kernel, out_shape=jax.ShapeDtypeStruct((RING * snaps,...  22.1 us
    pallas_call x1, Pallas kernels, local(): pl.pallas_call(prep_kernel, out_shape=(jax.ShapeDtypeStruct((8, 128), jnp...  4.84 us

profile of v1, /device:TPU:0, one launch (start us, length us, event | category | flops | bytes accessed | tf_op | source)
XLA Modules:
  0.0 185.2 jit_solution(2377130493653475640)
XLA Ops:
  0.0 0.0 copy-start.2
  0.0 0.0 copy-start.1
  0.0 0.0 copy-start.3
  0.0 0.0 copy-start.4
  0.0 0.8 copy.15
  0.8 0.6 reshape.13.counts
  1.4 1.4 copy.14
  2.8 4.8 %rank_entries.1 = (s32[8,128]{1,0:T(8,128)}, s32[96]{0:T(128)}, s32[16,4]{1,0:T(8,128)}) custom-call(s32[16,4]{1,0:T(8,128)} %bitcast.7, s32[16]{0:T(128)} %reshape.13.counts), custom_call_target="tpu_custom_call" | custom-call | tf_op jit(solution)/shard_map/rank_entries/pallas_call | solution.py:340
  7.6 154.2 %fetch_attend.1.arr = bf16[32,64,256]{2,1,0:T(8,128)(2,1)} custom-call(s32[8,128]{1,0:T(8,128)} %get-tuple-element.8.req, s32[96]{0:T(128)} %get-tuple-element.9.blk, s32[16,4]{1,0:T(8,128)} %get-tuple-element.10.table, s32[8,1,128]{2,1,0:T(1,128)} %bitcast.8, bf16[16,128,256]{2,1,0:T(8,128)(2,1)} %bitcast.6, bf16[256,256]{1,0:T(8,128)(2,1)} %wq_in.1, ...), custom_call_target="tpu_custom_call" | custom-call | tf_op jit(solution)/shard_map/fetch_attend/pallas_call | solution.py:353
  161.8 0.0 copy-done.2
  161.8 0.0 copy-done.1
  161.8 0.0 copy-done.3
  161.8 0.0 copy-done.4
  161.8 0.0 copy-start
  161.9 1.2 copy-done
  163.1 22.1 %attend_time.1 = f32[32,64,256]{2,1,0:T(8,128)} custom-call(s32[256]{0:T(256)S(1)} %copy-done.4, bf16[32,64,256]{2,1,0:T(8,128)(2,1)S(1)} %copy-done, bf16[32,256]{1,0:T(8,128)(2,1)S(1)} %copy-done.3, bf16[256,768]{1,0:T(8,128)(2,1)S(1)} %copy-done.1, bf16[256,256]{1,0:T(8,128)(2,1)S(1)} %copy-done.2), custom_call_target="tpu_custom_call" | custom-call | tf_op jit(solution)/shard_map/attend_time/pallas_call | solution.py:381
Async XLA Ops:
  0.0 161.8 %copy-start.2 = (bf16[256,256]{1,0:T(8,128)(2,1)S(1)}, bf16[256,256]{1,0:T(8,128)(2,1)}, u32[]{:S(2)}) copy-start(bf16[256,256]{1,0:T(8,128)(2,1)} %wo.1) | copy-start | bytes 393220
  0.0 161.8 %copy-start.1 = (bf16[256,768]{1,0:T(8,128)(2,1)S(1)}, bf16[256,768]{1,0:T(8,128)(2,1)}, u32[]{:S(2)}) copy-start(bf16[256,768]{1,0:T(8,128)(2,1)} %wqkv.1) | copy-start | bytes 1179652
  0.0 161.8 %copy-start.3 = (bf16[32,256]{1,0:T(8,128)(2,1)S(1)}, bf16[32,256]{1,0:T(8,128)(2,1)}, u32[]{:S(2)}) copy-start(bf16[32,256]{1,0:T(8,128)(2,1)} %pos.1) | copy-start | bytes 49156
  0.0 161.8 %copy-start.4 = (s32[256]{0:T(256)S(1)}, s32[256]{0:T(256)}, u32[]{:S(2)}) copy-start(s32[256]{0:T(256)} %births.1) | copy-start | bytes 3076
  161.8 1.2 copy-start

commit v2 on v1

--- a/solution.py
+++ b/solution.py
@@ -154,14 +154,8 @@
     @pl.loop(0, BLOCKS)
     def _(b):
         q = (dot(wt[0], feat[b], NT) * SCALE).astype(jnp.bfloat16)
-        zero = jnp.zeros((HS, TILE), jnp.bfloat16)
-        for h in range(HEADS):
-            p, lo = h // 2, (h % 2) * TILE
-            base = (h % 4) * HS
-            for g in range(4):
-                if g != h % 4:
-                    wq[b, p, g * HS : (g + 1) * HS, lo : lo + TILE] = zero
-            wq[b, p, base : base + HS, lo : lo + TILE] = q[h * HS : (h + 1) * HS]
+        wq[b, 0] = q[:TILE]
+        wq[b, 1] = q[TILE:]
 
     for row in range(1, 8):
         ask(row).wait()
@@ -193,36 +187,40 @@
         for r in range(RANKS):
             recv[0, j, r] = source[req[0, j * RANKS + r]]
 
-    def attend(row, j, r):
+    lane_head = lax.broadcasted_iota(jnp.int32, (1, TILE), 1) // HS
+    masks = [(lane_head == g).astype(jnp.float32).astype(jnp.bfloat16) for g in range(4)]
+
+    def attend3(row, j):
+        rows3 = recv[row, j].reshape(RANKS * TILE, D)
+        keys3 = dot(rows3, wkv_in[:, :D]).astype(jnp.bfloat16)
+        values3 = dot(wt[1], rows3, NT).astype(jnp.bfloat16)
+        for r in range(RANKS):
+            attend(row, j, r, keys3[r * TILE : (r + 1) * TILE], values3[:, r * TILE : (r + 1) * TILE])
+
+    def attend(row, j, r, keys, values):
         n = (row * RING + j) * RANKS + r
         b = blk[n]
-        rows = recv[row, j, r]
-        keys = dot(rows, wkv_in[:, :D]).astype(jnp.bfloat16)
-        values = dot(wt[1], rows, NT).astype(jnp.bfloat16)
-        for p in range(HEADS // 2):
-            half = (p // 2) * TILE
-            s = dot(keys[:, half : half + TILE], wq[b, p])
-            m = jnp.max(s, axis=0, keepdims=True)
-            e = jnp.exp2(s - m)
-            t = jnp.sum(e, axis=0, keepdims=True)
-            o = dot(values[2 * p * HS : 2 * (p + 1) * HS], e.astype(jnp.bfloat16))
-            for g in range(2):
-                h = 2 * p + g
-                top[n, h : h + 1] = m[:, g * TILE : (g + 1) * TILE]
-                total[n, h : h + 1] = t[:, g * TILE : (g + 1) * TILE]
-                part[n, h * HS : (h + 1) * HS] = o[g * HS : (g + 1) * HS, g * TILE : (g + 1) * TILE]
+
+        for half in range(2):
+            kh = keys[:, half * TILE : (half + 1) * TILE]
+            s = dot(jnp.concatenate([kh * w for w in masks], axis=0), wq[b, half])
+            s = s.reshape(4, TILE, TILE)
+            m = jnp.max(s, axis=1)
+            e = jnp.exp2(s - m[:, None])
+            top[n, half * 4 : half * 4 + 4] = m
+            total[n, half * 4 : half * 4 + 4] = jnp.sum(e, axis=1)
+            e = e.astype(jnp.bfloat16)
+            for g in range(4):
+                h = half * 4 + g
+                part[n, h * HS : (h + 1) * HS] = dot(values[h * HS : (h + 1) * HS], e[g])
 
     for j in ORDER:
-        for r in range(RANKS):
-            attend(0, j, r)
+        attend3(0, j)
 
         @pl.loop(1, 8)
         def _(row):
             send(row, j).wait_recv()
-
-            @pl.loop(0, RANKS)
-            def _(r):
-                attend(row, j, r)
+            attend3(row, j)
 
     def spread(i, half):
         group = (y + i) % RING
@@ -363,7 +361,7 @@
             pltpu.VMEM((BLOCKS, TILE, width), half),
             pltpu.VMEM((8, RING, RANKS, TILE, width), half),
             pltpu.VMEM((8, RING, RANKS, TILE, width), half),
-            pltpu.VMEM((BLOCKS, HEADS // 2, TILE, 2 * TILE), half),
+            pltpu.VMEM((BLOCKS, 2, TILE, TILE), half),
             pltpu.VMEM((2, width, width), half),
             pltpu.VMEM((SLOTS, width, TILE), jnp.float32),
             pltpu.VMEM((SLOTS, HEADS, TILE), jnp.float32),

time: 185 us -> 130 us (0.70)
  Pallas kernels: 181 us -> 126 us
    pallas_call x1, Pallas kernels: 154 us -> 99.1 us  [local(): pl.pallas_call(fetch_kernel, out_shape=jax.ShapeDtypeStruct((RING * snaps...]
where the time goes in v2:
time: 130 us
  Pallas kernels  126 us (97%)
  local copies, waits for them, and re-layouts  3.99 us (3%)
    pallas_call x1, Pallas kernels, local(): pl.pallas_call(fetch_kernel, out_shape=jax.ShapeDtypeStruct((RING * snaps...  99.1 us
    pallas_call x1, Pallas kernels, local(): pl.pallas_call(time_kernel, out_shape=jax.ShapeDtypeStruct((RING * snaps,...  22.1 us
    pallas_call x1, Pallas kernels, local(): pl.pallas_call(prep_kernel, out_shape=(jax.ShapeDtypeStruct((8, 128), jnp...  4.84 us
    unnamed x12, local copies, waits for them, and re-layouts  3.41 us

profile of v2, /device:TPU:0, one launch (start us, length us, event | category | flops | bytes accessed | tf_op | source)
XLA Modules:
  0.0 130.1 jit_solution(325879915222583801)
XLA Ops:
  0.0 0.0 copy-start.2
  0.0 0.0 copy-start.1
  0.0 0.0 copy-start.3
  0.0 0.0 copy-start.4
  0.0 0.8 copy.15
  0.8 0.6 reshape.13.counts
  1.4 1.4 %copy.14 = s32[8,2,4]{2,1,0:T(2,128)} copy(s32[8,2,4]{0,2,1:T(4,128)} %param.11) | data formatting | bytes 512 | tf_op args[1]
  2.8 4.8 %rank_entries.1 = (s32[8,128]{1,0:T(8,128)}, s32[96]{0:T(128)}, s32[16,4]{1,0:T(8,128)}) custom-call(s32[16,4]{1,0:T(8,128)} %bitcast.7, s32[16]{0:T(128)} %reshape.13.counts), custom_call_target="tpu_custom_call" | custom-call | tf_op jit(solution)/shard_map/rank_entries/pallas_call | solution.py:338
  7.6 99.1 %fetch_attend.1.arr = bf16[32,64,256]{2,1,0:T(8,128)(2,1)} custom-call(s32[8,128]{1,0:T(8,128)} %get-tuple-element.8.req, s32[96]{0:T(128)} %get-tuple-element.9.blk, s32[16,4]{1,0:T(8,128)} %get-tuple-element.10.table, s32[8,1,128]{2,1,0:T(1,128)} %bitcast.8, bf16[16,128,256]{2,1,0:T(8,128)(2,1)} %bitcast.6, bf16[256,256]{1,0:T(8,128)(2,1)} %wq_in.1, ...), custom_call_target="tpu_custom_call" | custom-call | tf_op jit(solution)/shard_map/fetch_attend/pallas_call | solution.py:351
  106.7 0.0 copy-done.2
  106.7 0.0 copy-done.1
  106.8 0.0 copy-done.3
  106.8 0.0 copy-done.4
  106.8 0.0 copy-start
  106.8 1.2 copy-done
  108.0 22.1 %attend_time.1 = f32[32,64,256]{2,1,0:T(8,128)} custom-call(s32[256]{0:T(256)S(1)} %copy-done.4, bf16[32,64,256]{2,1,0:T(8,128)(2,1)S(1)} %copy-done, bf16[32,256]{1,0:T(8,128)(2,1)S(1)} %copy-done.3, bf16[256,768]{1,0:T(8,128)(2,1)S(1)} %copy-done.1, bf16[256,256]{1,0:T(8,128)(2,1)S(1)} %copy-done.2), custom_call_target="tpu_custom_call" | custom-call | tf_op jit(solution)/shard_map/attend_time/pallas_call | solution.py:379
Async XLA Ops:
  0.0 106.7 %copy-start.2 = (bf16[256,256]{1,0:T(8,128)(2,1)S(1)}, bf16[256,256]{1,0:T(8,128)(2,1)}, u32[]{:S(2)}) copy-start(bf16[256,256]{1,0:T(8,128)(2,1)} %wo.1) | copy-start | bytes 393220
  0.0 106.7 %copy-start.1 = (bf16[256,768]{1,0:T(8,128)(2,1)S(1)}, bf16[256,768]{1,0:T(8,128)(2,1)}, u32[]{:S(2)}) copy-start(bf16[256,768]{1,0:T(8,128)(2,1)} %wqkv.1) | copy-start | bytes 1179652
  0.0 106.8 %copy-start.3 = (bf16[32,256]{1,0:T(8,128)(2,1)S(1)}, bf16[32,256]{1,0:T(8,128)(2,1)}, u32[]{:S(2)}) copy-start(bf16[32,256]{1,0:T(8,128)(2,1)} %pos.1) | copy-start | bytes 49156
  0.0 106.8 %copy-start.4 = (s32[256]{0:T(256)S(1)}, s32[256]{0:T(256)}, u32[]{:S(2)}) copy-start(s32[256]{0:T(256)} %births.1) | copy-start | bytes 3076
  106.8 1.2 copy-start

commit v3 on v2

v3 whole, which is shorter than its diff:
```python
import functools

import jax
import jax.numpy as jnp
from jax import lax
from jax.experimental import pallas as pl
from jax.experimental.pallas import tpu as pltpu
from jax.sharding import PartitionSpec as P

HEADS = 8
TILE = 128
D = 256
HS = D // HEADS
KT = 4
BLOCKS = 16
RING = 4
RANKS = 3
SLOTS = 2 * RING * RING * RANKS
SCALE = 1.4426950408889634 * HS**-0.5
MESH = pl.DeviceIdType.MESH
NT = (((1,), (1,)), ((), ()))
TN = (((0,), (0,)), ((), ()))
NN = (((1,), (0,)), ((), ()))


def dot(a, b, dims=NN):
    return lax.dot_general(a, b, dims, preferred_element_type=jnp.float32)


def vert_id(z, x, core):
    return (z * RING + x) * 2 + core


def position():
    v = lax.axis_index("vert")
    return v // (2 * RING), (v // 2) % RING, v % 2


def make_plan(cols, counts, z, x, core, plan_v):
    shape = (TILE, TILE)
    lane = lax.broadcasted_iota(jnp.int32, (1, TILE), 1)
    col = jnp.full((1, TILE), -1, jnp.int32)
    for n in range(BLOCKS * KT):
        s, u, k = n // 8, (n // 4) % 2, n % 4
        col = jnp.where(lane == n, jnp.where(k < counts[s, u], cols[s, u, k], -1), col)
    owner = jnp.maximum(col, 0) >> 1
    oz, ox, oc = owner >> 3, (owner >> 1) & 3, owner & 1
    i = jnp.where(oc == 0, x - ox, z - oz) & 3
    j = jnp.where(oc == 0, oz - z, ox - x) & 3
    base = (jnp.where(oc == core, 0, RING) + i) * RING + j
    base = jnp.where(col >= 0, base, -1)
    base_down = jnp.broadcast_to(base, shape).T
    n_down = lax.broadcasted_iota(jnp.int32, shape, 0)
    n_across = lax.broadcasted_iota(jnp.int32, shape, 1)
    before = (base_down == base) & (n_down < n_across)
    rank = jnp.sum(jnp.where(before, 1, 0), axis=0, keepdims=True)
    place = jnp.where(base >= 0, base * RANKS + rank, -1)
    place_down = jnp.broadcast_to(place, shape).T
    code = ((lane >> 3) << 1) + (jnp.maximum(col, 0) & 1)
    code_down = jnp.broadcast_to(code, shape).T
    plan_v[16] = place
    per = RING * RANKS
    for row in range(8):
        hit = (place_down == n_across + row * per) & (n_across < per)
        plan_v[row] = jnp.sum(jnp.where(hit, code_down, 0), axis=0, keepdims=True)
        plan_v[8 + row] = jnp.sum(jnp.where(hit, n_down >> 2, 0), axis=0, keepdims=True)


def graph_kernel(
    cols, counts, births, feat, wq_in, wkv_in, wso, pos, wqkv, wo, out,
    plan_v, plan, codes_v, codes, ag1, ag2, ag3, stage, recv, wq, wt, turn_s, part, top, total, hid, arr, held,
    req_send, req_recv, loc_sem, ag_send, ag_recv, tile_send, tile_recv, snap_send, snap_recv, own_sem, out_sem,
):
    z, x, core = position()
    y = lax.axis_index("snap")
    flat = core == 0

    def gather_peer(j):
        return vert_id(
            jnp.where(flat, (z + j) % RING, z), jnp.where(flat, x, (x + j) % RING), core
        )

    def dest(row):
        i = row % RING
        other = row // RING
        return vert_id(
            jnp.where(flat, z, (z + i) % RING),
            jnp.where(flat, (x + i) % RING, x),
            (core + other) % 2,
        )

    def relay(row):
        i = row % RING
        c = (core + row // RING) % 2
        return vert_id(
            jnp.where(c == 0, z, (z + RING - i) % RING),
            jnp.where(c == 0, (x + RING - i) % RING, x),
            c,
        )

    barrier = pltpu.get_barrier_semaphore()
    greet = [gather_peer(1), gather_peer(2), gather_peer(3)]
    greet += [dest(r) for r in range(1, 8)]
    greet += [relay(r) for r in range(5, 8)]
    for v in greet:
        pl.semaphore_signal(barrier, inc=1, device_id=(y, v), device_id_type=MESH)
    for i in range(1, RING):
        pl.semaphore_signal(
            barrier, inc=1, device_id=((y + i) % RING, lax.axis_index("vert")), device_id_type=MESH
        )
    pl.semaphore_wait(barrier, len(greet) + RING - 1)

    gathered = {1: ag1, 2: ag2, 3: ag3}
    lower, upper = pl.ds(0, 8), pl.ds(8, 8)

    def share(j, half):
        rows = upper if half else lower
        source = (ag3 if half else ag1) if j == 2 else feat
        there = gather_peer((1 if half else 3) if j == 2 else RING - j)
        return pltpu.make_async_remote_copy(
            src_ref=source.at[rows],
            dst_ref=gathered[j].at[rows],
            send_sem=ag_send.at[j - 1, half],
            recv_sem=ag_recv.at[j - 1, half],
            device_id=(y, there),
            device_id_type=MESH,
        )

    share(1, 0).start()
    share(3, 1).start()
    share(1, 1).start()
    share(3, 0).start()

    make_plan(cols, counts, z, x, core, plan_v)

    def ask(row):
        return pltpu.make_async_remote_copy(
            src_ref=plan_v.at[row],
            dst_ref=codes_v.at[row],
            send_sem=req_send.at[row],
            recv_sem=req_recv.at[row],
            device_id=(y, relay(row)),
            device_id_type=MESH,
        )

    for row in range(1, 8):
        ask(row).start()
    mine_down = pltpu.make_async_copy(plan_v, plan, own_sem)
    mine_down.start()

    wt[0] = wq_in[...].astype(jnp.float32).T.astype(jnp.bfloat16)
    wt[1] = wkv_in[:, D:].astype(jnp.float32).T.astype(jnp.bfloat16)

    @pl.loop(0, BLOCKS)
    def _(b):
        q = (dot(wt[0], feat[b], NT) * SCALE).astype(jnp.bfloat16)
        wq[b, 0] = q[:TILE]
        wq[b, 1] = q[TILE:]

    mine_down.wait()
    for row in range(1, 8):
        ask(row).wait()
    down = pltpu.make_async_copy(codes_v.at[pl.ds(1, 7)], codes.at[pl.ds(1, 7)], loc_sem)
    down.start()
    down.wait()

    def send(row, j):
        return pltpu.make_async_remote_copy(
            src_ref=stage.at[row, j],
            dst_ref=recv.at[row, j],
            send_sem=tile_send.at[row, j],
            recv_sem=tile_recv.at[row, j],
            device_id=(y, dest(row)),
            device_id_type=MESH,
        )

    def pass_on(j):
        source = gathered[j] if j else feat

        @pl.loop(1, 8)
        def _(row):
            for r in range(RANKS):
                stage[row, j, r] = source[codes[row, 0, j * RANKS + r]]
            send(row, j).start()

        for r in range(RANKS):
            recv[0, j, r] = source[plan[0, 0, j * RANKS + r]]

    lane_head = lax.broadcasted_iota(jnp.int32, (1, TILE), 1) // HS
    masks = [(lane_head == g).astype(jnp.float32).astype(jnp.bfloat16) for g in range(4)]

    def attend3(row, j):
        rows3 = recv[row, j].reshape(RANKS * TILE, D)
        keys3 = dot(rows3, wkv_in[:, :D]).astype(jnp.bfloat16)
        values3 = dot(wt[1], rows3, NT).astype(jnp.bfloat16)
        for r in range(RANKS):
            attend(row, j, r, keys3[r * TILE : (r + 1) * TILE], values3[:, r * TILE : (r + 1) * TILE])

    def attend(row, j, r, keys, values):
        n = (row * RING + j) * RANKS + r
        b = plan[8 + row, 0, j * RANKS + r]

        for half in range(2):
            kh = keys[:, half * TILE : (half + 1) * TILE]
            s = dot(jnp.concatenate([kh * w for w in masks], axis=0), wq[b, half])
            s = s.reshape(4, TILE, TILE)
            m = jnp.max(s, axis=1)
            e = jnp.exp2(s - m[:, None])
            top[n, half * 4 : half * 4 + 4] = m
            total[n, half * 4 : half * 4 + 4] = jnp.sum(e, axis=1)
            e = e.astype(jnp.bfloat16)
            for g in range(4):
                h = half * 4 + g
                part[n, h * HS : (h + 1) * HS] = dot(values[h * HS : (h + 1) * HS], e[g])

    def attend_rows(j, first, last):
        @pl.loop(first, last)
        def _(row):
            send(row, j).wait_recv()
            attend3(row, j)

    def attend_own(j):
        @pl.loop(0, 1)
        def _(row):
            attend3(row, j)

    pass_on(0)
    share(1, 0).wait_recv()
    share(2, 0).start()
    share(3, 1).wait_recv()
    share(2, 1).start()
    attend_own(0)
    share(1, 1).wait_recv()
    pass_on(1)
    share(3, 0).wait_recv()
    pass_on(3)
    attend_own(1)
    attend_own(3)
    attend_rows(0, 1, 4)
    share(2, 0).wait_recv()
    share(2, 1).wait_recv()
    pass_on(2)

    wt[2] = wqkv[:, :D].astype(jnp.float32).T.astype(jnp.bfloat16)
    wt[3] = wqkv[:, 2 * D :].astype(jnp.float32).T.astype(jnp.bfloat16)
    snaps = pos.shape[0]
    n = snaps * 8
    to = lax.broadcasted_iota(jnp.int32, (n, n), 0)
    source = lax.broadcasted_iota(jnp.int32, (n, n), 1)
    turn_s[0] = ((to % snaps) * 8 + to // snaps == source).astype(jnp.float32).astype(jnp.bfloat16)
    turn_s[1] = ((source % snaps) * 8 + source // snaps == to).astype(jnp.float32).astype(jnp.bfloat16)

    attend_rows(0, 4, 8)
    attend_own(2)
    attend_rows(1, 1, 8)
    attend_rows(3, 1, 8)
    attend_rows(2, 1, 8)

    @pl.loop(0, 8)
    def _(s):
        for u in range(2):
            b = s * 2 + u
            slots, live, tops = [], [], []
            for k in range(KT):
                slot = plan[16, 0, b * KT + k]
                alive = slot >= 0
                slot = jnp.where(alive, slot, 0)
                slots.append(slot)
                live.append(jnp.where(alive, jnp.float32(0), jnp.float32(-jnp.inf)))
                tops.append(top[slot] + live[k])
            m = functools.reduce(jnp.maximum, tops)
            weights = [jnp.exp2(t - m) for t in tops]
            denominator = sum(weights[k] * total[slots[k]] for k in range(KT))
            weights = [w / denominator for w in weights]
            parts = []
            for h in range(HEADS):
                parts.append(
                    sum(
                        weights[k][h : h + 1] * part[slots[k], h * HS : (h + 1) * HS]
                        for k in range(KT)
                    )
                )
            attended = jnp.concatenate(parts, axis=0).T.astype(jnp.bfloat16)
            update = dot(attended, wso[...])
            hid[s, u * TILE : (u + 1) * TILE] = (feat[b].astype(jnp.float32) + update).astype(
                jnp.bfloat16
            )


    def spread(i, chunk):
        group = (y + i) % RING
        return pltpu.make_async_remote_copy(
            src_ref=hid.at[:, pl.ds(group * 64 + chunk * 16, 16)],
            dst_ref=arr.at[pl.ds(y * 8, 8), pl.ds(chunk * 16, 16)],
            send_sem=snap_send.at[chunk, i],
            recv_sem=snap_recv.at[chunk, i],
            device_id=(group, lax.axis_index("vert")),
            device_id_type=MESH,
        )

    for chunk in range(4):
        for i in (2, 1, 3):
            spread(i, chunk).start()
    arr[pl.ds(y * 8, 8)] = hid[:, pl.ds(y * 64, 64)]

    lane = lax.broadcasted_iota(jnp.int32, (1, 1, TILE), 2)
    key_snap = lax.broadcasted_iota(jnp.int32, (1, snaps, 1), 1)
    query_snap = lane % snaps
    own_lane = [lane // snaps == v for v in range(4)]
    positions = pos[...].astype(jnp.float32)[:, None, :]

    def write(step):
        return pltpu.make_async_copy(held.at[step], out.at[:, pl.ds(step * 16, 16)], out_sem.at[step])

    @pl.loop(0, 4)
    def _(step):
        for i in range(1, RING):
            spread(i, step).wait_recv()
        hidden = arr[:, pl.ds(step * 16, 16)].astype(jnp.float32)
        for g in range(2):
            base = y * 64 + step * 16 + g * 8
            mine = hidden[:, g * 8 : (g + 1) * 8]
            rows = (mine + positions).reshape(n, D).astype(jnp.bfloat16)
            rows = dot(turn_s[0], rows).astype(jnp.bfloat16)
            q = (dot(wt[2], rows, NT) * SCALE).astype(jnp.bfloat16)
            keys = dot(rows, wqkv[:, D : 2 * D]).astype(jnp.bfloat16)
            values = dot(wt[3], rows, NT).astype(jnp.bfloat16)
            sides = []
            for u in range(2):
                birth = jnp.zeros((1, 1, TILE), jnp.int32)
                for v in range(4):
                    birth = jnp.where(own_lane[v], births[base + u * 4 + v], birth)
                allowed = (query_snap == key_snap) | ((query_snap >= key_snap) & (key_snap >= birth))
                bias = jnp.where(allowed, jnp.float32(0), jnp.float32(-jnp.inf))
                mixed = []
                for half in range(2):
                    kh = keys[u * TILE : (u + 1) * TILE, half * TILE : (half + 1) * TILE]
                    qh = q[half * TILE : (half + 1) * TILE, u * TILE : (u + 1) * TILE]
                    s = dot(jnp.concatenate([kh * w for w in masks], axis=0), qh)
                    s = s.reshape(4, 4, snaps, TILE)
                    near = s[:, 0]
                    for v in range(1, 4):
                        near = jnp.where(own_lane[v], s[:, v], near)
                    near = near + bias
                    m = jnp.max(near, axis=1, keepdims=True)
                    e = jnp.exp2(near - m)
                    t = jnp.sum(e, axis=1, keepdims=True)
                    for h in range(4):
                        wide = jnp.concatenate(
                            [jnp.where(own_lane[v][0], e[h], 0.0) for v in range(4)], axis=0
                        ).astype(jnp.bfloat16)
                        top = (half * 4 + h) * HS
                        o = dot(values[top : top + HS, u * TILE : (u + 1) * TILE], wide)
                        mixed.append((o / t[h]).astype(jnp.bfloat16))
                sides.append(jnp.concatenate(mixed, axis=0))
            mixed = dot(turn_s[1], jnp.concatenate(sides, axis=1), NT).astype(jnp.bfloat16)
            held[step, :, g * 8 : (g + 1) * 8] = mine + dot(mixed, wo[...]).reshape(snaps, 8, D)
        write(step).start()

    for chunk in range(4):
        write(chunk).wait()
        for i in range(1, RING):
            spread(i, chunk).wait_send()
    for j, half in ((1, 0), (1, 1), (2, 0), (2, 1), (3, 0), (3, 1)):
        share(j, half).wait_send()
    for j in range(RING):

        @pl.loop(1, 8)
        def _(row):
            send(row, j).wait_send()


def local(features, tile_cols, counts, births, wq, wkv, wso, pos, wqkv, wo):
    snaps, rows, width = features.shape
    smem = pl.BlockSpec(memory_space=pltpu.SMEM)
    vmem = pl.BlockSpec(memory_space=pltpu.VMEM)
    dma = pltpu.SemaphoreType.DMA
    half = jnp.bfloat16
    count = rows // RING
    result = pl.pallas_call(
        graph_kernel,
        out_shape=jax.ShapeDtypeStruct((RING * snaps, count, width), jnp.float32),
        in_specs=[smem] * 3 + [vmem] * 7,
        out_specs=pl.BlockSpec(memory_space=pl.ANY),
        scratch_shapes=[
            pltpu.VMEM((17, 1, TILE), jnp.int32),
            pltpu.SMEM((17, 1, TILE), jnp.int32),
            pltpu.VMEM((8, 1, TILE), jnp.int32),
            pltpu.SMEM((8, 1, TILE), jnp.int32),
            pltpu.VMEM((BLOCKS, TILE, width), half),
            pltpu.VMEM((BLOCKS, TILE, width), half),
            pltpu.VMEM((BLOCKS, TILE, width), half),
            pltpu.VMEM((8, RING, RANKS, TILE, width), half),
            pltpu.VMEM((8, RING, RANKS, TILE, width), half),
            pltpu.VMEM((BLOCKS, 2, TILE, TILE), half),
            pltpu.VMEM((4, width, width), half),
            pltpu.VMEM((2, RING * snaps * 8, RING * snaps * 8), half),
            pltpu.VMEM((SLOTS, width, TILE), jnp.float32),
            pltpu.VMEM((SLOTS, HEADS, TILE), jnp.float32),
            pltpu.VMEM((SLOTS, HEADS, TILE), jnp.float32),
            pltpu.VMEM((snaps, rows, width), half),
            pltpu.VMEM((RING * snaps, count, width), half),
            pltpu.VMEM((RING, RING * snaps, 16, width), jnp.float32),
            dma((8,)), dma((8,)), dma, dma((3, 2)), dma((3, 2)),
            dma((8, RING)), dma((8, RING)), dma((4, RING)), dma((4, RING)), dma, dma((4,)),
        ],
        compiler_params=pltpu.CompilerParams(
            collective_id=0, has_side_effects=True, vmem_limit_bytes=56 * 2**20
        ),
        name="graph",
    )(tile_cols, counts, births, features.reshape(BLOCKS, TILE, width), wq, wkv, wso, pos, wqkv, wo)
    return result[:, None, None]


def solution(mesh):
    placed = (
        P("snap", "vert", None), P("snap", "vert", None), P("snap", "vert"), P("vert"),
        P(), P(), P(), P(), P(), P(),
    )
    return jax.shard_map(
        local,
        mesh=mesh,
        in_specs=placed,
        out_specs=P(None, "vert", "snap", None, None),
        check_vma=False,
    )
```

time: 130 us -> 96.8 us (0.74); the launches traced: 130 us -> 95.3 us
  Pallas kernels: 126 us -> 89.4 us
  local copies, waits for them, and re-layouts: 3.99 us -> 5.84 us
    pallas_call x3 -> x1, Pallas kernels: 126 us -> 89.4 us  [local(): pl.pallas_call(graph_kernel, out_shape=jax.ShapeDtypeStruct((RING * snaps...]
    unnamed x12 -> x3, local copies, waits for them, and re-layouts: 3.41 us -> 5.84 us
where the time goes in v3:
time: 96.8 us; the launch traced here: 95.3 us
  Pallas kernels  89.4 us (92%)
  local copies, waits for them, and re-layouts  5.84 us (6%)
    pallas_call x1, Pallas kernels, local(): pl.pallas_call(graph_kernel, out_shape=jax.ShapeDtypeStruct((RING * snaps...  89.4 us
    unnamed x3, local copies, waits for them, and re-layouts  5.84 us

profile of v3, /device:TPU:0, one launch (start us, length us, event | category | flops | bytes accessed | tf_op | source)
XLA Modules:
  0.0 95.3 jit_solution(9483235510066930770)
XLA Ops:
  0.0 1.3 %copy.12.counts = s32[8,2]{1,0:T(8,128)} copy(s32[8,2]{0,1:T(2,128)} %param.12) | data formatting | bytes 128 | tf_op args[2]
  1.3 1.4 %copy.11.cols = s32[8,2,4]{2,1,0:T(2,128)} copy(s32[8,2,4]{0,2,1:T(4,128)} %param.11) | data formatting | bytes 512 | tf_op args[1]
  2.7 89.4 %graph.1 = f32[32,64,256]{2,1,0:T(8,128)} custom-call(s32[8,2,4]{2,1,0:T(2,128)} %copy.11.cols, s32[8,2]{1,0:T(8,128)} %copy.12.counts, s32[256]{0:T(256)} %births.1, bf16[16,128,256]{2,1,0:T(8,128)(2,1)} %bitcast.5, bf16[256,256]{1,0:T(8,128)(2,1)} %wq_in.1, bf16[256,512]{1,0:T(8,128)(2,1)} %wkv_in.1, bf16[256,256]{1,0:T(8,128)(2,1)} %wso.1, ...), custom_call_target="tpu_custom_call" | custom-call | tf_op jit(solution)/shard_map/graph/pallas_call | solution.py:380
  92.1 3.1 %copy.15 = f32[32,1,1,64,256]{4,3,2,1,0:T(8,128)} copy(f32[32,1,1,64,256]{4,3,2,1,0:T(8,128)} %bitcast.4) | data formatting | bytes 4194304

commit v4 on v3

--- a/solution.py
+++ b/solution.py
@@ -42,7 +42,7 @@
     col = jnp.full((1, TILE), -1, jnp.int32)
     for n in range(BLOCKS * KT):
         s, u, k = n // 8, (n // 4) % 2, n % 4
-        col = jnp.where(lane == n, jnp.where(k < counts[s, u], cols[s, u, k], -1), col)
+        col = jnp.where(lane == n, jnp.where(k < counts[u, s], cols[u, k, s], -1), col)
     owner = jnp.maximum(col, 0) >> 1
     oz, ox, oc = owner >> 3, (owner >> 1) & 3, owner & 1
     i = jnp.where(oc == 0, x - ox, z - oz) & 3
@@ -67,9 +67,10 @@
 
 
 def graph_kernel(
-    cols, counts, births, feat, wq_in, wkv_in, wso, pos, wqkv, wo, out,
+    cols_in, counts_in, births_in, feat_in, wq_hbm, wkv_hbm, wso_hbm, pos_hbm, wqkv_hbm, wo_hbm, out,
+    cols, counts, births, feat, wq_in, wkv_in, wso, pos, wqkv, wo,
     plan_v, plan, codes_v, codes, ag1, ag2, ag3, stage, recv, wq, wt, turn_s, part, top, total, hid, arr, held,
-    req_send, req_recv, loc_sem, ag_send, ag_recv, tile_send, tile_recv, snap_send, snap_recv, own_sem, out_sem,
+    req_send, req_recv, loc_sem, ag_send, ag_recv, tile_send, tile_recv, snap_send, snap_recv, own_sem, out_sem, in_sem,
 ):
     z, x, core = position()
     y = lax.axis_index("snap")
@@ -98,6 +99,17 @@
             c,
         )
 
+    held_here = [
+        pltpu.make_async_copy(there, here, in_sem.at[at])
+        for at, (there, here) in enumerate(
+            (
+                (cols_in, cols), (counts_in, counts), (births_in, births), (wq_hbm, wq_in), (feat_in, feat),
+                (wkv_hbm, wkv_in), (wso_hbm, wso), (pos_hbm, pos), (wqkv_hbm, wqkv), (wo_hbm, wo),
+            )
+        )
+    ]
+    for copy in held_here:
+        copy.start()
     barrier = pltpu.get_barrier_semaphore()
     greet = [gather_peer(1), gather_peer(2), gather_peer(3)]
     greet += [dest(r) for r in range(1, 8)]
@@ -108,14 +120,30 @@
         pl.semaphore_signal(
             barrier, inc=1, device_id=((y + i) % RING, lax.axis_index("vert")), device_id_type=MESH
         )
+    held_here[0].wait()
+    held_here[1].wait()
+    make_plan(cols, counts, z, x, core, plan_v)
     pl.semaphore_wait(barrier, len(greet) + RING - 1)
+
+    def ask(row):
+        return pltpu.make_async_remote_copy(
+            src_ref=plan_v.at[row],
+            dst_ref=codes_v.at[row],
+            send_sem=req_send.at[row],
+            recv_sem=req_recv.at[row],
+            device_id=(y, relay(row)),
+            device_id_type=MESH,
+        )
+
+    for row in range(1, 8):
+        ask(row).start()
 
     gathered = {1: ag1, 2: ag2, 3: ag3}
     lower, upper = pl.ds(0, 8), pl.ds(8, 8)
 
     def share(j, half):
         rows = upper if half else lower
-        source = (ag3 if half else ag1) if j == 2 else feat
+        source = (ag3 if half else ag1) if j == 2 else feat_in
         there = gather_peer((1 if half else 3) if j == 2 else RING - j)
         return pltpu.make_async_remote_copy(
             src_ref=source.at[rows],
@@ -131,31 +159,8 @@
     share(1, 1).start()
     share(3, 0).start()
 
-    make_plan(cols, counts, z, x, core, plan_v)
-
-    def ask(row):
-        return pltpu.make_async_remote_copy(
-            src_ref=plan_v.at[row],
-            dst_ref=codes_v.at[row],
-            send_sem=req_send.at[row],
-            recv_sem=req_recv.at[row],
-            device_id=(y, relay(row)),
-            device_id_type=MESH,
-        )
-
-    for row in range(1, 8):
-        ask(row).start()
     mine_down = pltpu.make_async_copy(plan_v, plan, own_sem)
     mine_down.start()
-
-    wt[0] = wq_in[...].astype(jnp.float32).T.astype(jnp.bfloat16)
-    wt[1] = wkv_in[:, D:].astype(jnp.float32).T.astype(jnp.bfloat16)
-
-    @pl.loop(0, BLOCKS)
-    def _(b):
-        q = (dot(wt[0], feat[b], NT) * SCALE).astype(jnp.bfloat16)
-        wq[b, 0] = q[:TILE]
-        wq[b, 1] = q[TILE:]
 
     mine_down.wait()
     for row in range(1, 8):
@@ -200,43 +205,63 @@
         n = (row * RING + j) * RANKS + r
         b = plan[8 + row, 0, j * RANKS + r]
 
-        for half in range(2):
-            kh = keys[:, half * TILE : (half + 1) * TILE]
-            s = dot(jnp.concatenate([kh * w for w in masks], axis=0), wq[b, half])
-            s = s.reshape(4, TILE, TILE)
-            m = jnp.max(s, axis=1)
-            e = jnp.exp2(s - m[:, None])
-            top[n, half * 4 : half * 4 + 4] = m
-            total[n, half * 4 : half * 4 + 4] = jnp.sum(e, axis=1)
+        for g in range(4):
+            s = dot(keys * jnp.concatenate([masks[g], masks[g]], axis=1), wq[b])
+            m = jnp.max(s, axis=0, keepdims=True)
+            e = jnp.exp2(s - m)
+            t = jnp.sum(e, axis=0, keepdims=True)
             e = e.astype(jnp.bfloat16)
-            for g in range(4):
+            for half in range(2):
+                lanes = slice(half * TILE, (half + 1) * TILE)
                 h = half * 4 + g
-                part[n, h * HS : (h + 1) * HS] = dot(values[h * HS : (h + 1) * HS], e[g])
-
-    def attend_rows(j, first, last):
+                top[n, h : h + 1] = m[:, lanes]
+                total[n, h : h + 1] = t[:, lanes]
+                part[n, h * HS : (h + 1) * HS] = dot(values[h * HS : (h + 1) * HS], e[:, lanes])
+
+    def turn_of(t):
+        k = jnp.maximum(t - 8, 0)
+        pair = (k % 6) // 2
+        far = jnp.where(pair == 0, 1, jnp.where(pair == 1, 3, 2)) + RING * (k % 2)
+        near = jnp.where((t < 3) | (t == 6), 0, RING)
+        row = jnp.where(t < 8, near, far)
+        order = jnp.where(t < 3, t, jnp.where(t < 6, t - 3, jnp.where(t < 8, 3, k // 6)))
+        return row, jnp.where(order == 2, 3, jnp.where(order == 3, 2, order))
+
+    def attend_span(first, last):
         @pl.loop(first, last)
-        def _(row):
-            send(row, j).wait_recv()
+        def _(t):
+            row, j = turn_of(t)
+
+            @pl.when(row != 0)
+            def _():
+                send(row, j).wait_recv()
+
             attend3(row, j)
 
-    def attend_own(j):
-        @pl.loop(0, 1)
-        def _(row):
-            attend3(row, j)
-
-    pass_on(0)
+    for copy in held_here[2:]:
+        copy.wait()
+
+    wt[0] = wq_in[...].astype(jnp.float32).T.astype(jnp.bfloat16)
+    wt[1] = wkv_in[:, D:].astype(jnp.float32).T.astype(jnp.bfloat16)
+
+    @pl.loop(0, BLOCKS)
+    def _(b):
+        q = (dot(wt[0], feat[b], NT) * SCALE).astype(jnp.bfloat16)
+        wq[b, :TILE, :TILE] = q[:TILE]
+        wq[b, :TILE, TILE:] = jnp.zeros((TILE, TILE), jnp.bfloat16)
+        wq[b, TILE:, :TILE] = jnp.zeros((TILE, TILE), jnp.bfloat16)
+        wq[b, TILE:, TILE:] = q[TILE:]
+
     share(1, 0).wait_recv()
     share(2, 0).start()
     share(3, 1).wait_recv()
     share(2, 1).start()
-    attend_own(0)
     share(1, 1).wait_recv()
+    share(3, 0).wait_recv()
+    pass_on(0)
     pass_on(1)
-    share(3, 0).wait_recv()
     pass_on(3)
-    attend_own(1)
-    attend_own(3)
-    attend_rows(0, 1, 4)
+    attend_span(0, 3)
     share(2, 0).wait_recv()
     share(2, 1).wait_recv()
     pass_on(2)
@@ -250,11 +275,7 @@
     turn_s[0] = ((to % snaps) * 8 + to // snaps == source).astype(jnp.float32).astype(jnp.bfloat16)
     turn_s[1] = ((source % snaps) * 8 + source // snaps == to).astype(jnp.float32).astype(jnp.bfloat16)
 
-    attend_rows(0, 4, 8)
-    attend_own(2)
-    attend_rows(1, 1, 8)
-    attend_rows(3, 1, 8)
-    attend_rows(2, 1, 8)
+    attend_span(3, 32)
 
     @pl.loop(0, 8)
     def _(s):
@@ -372,17 +393,26 @@
 
 def local(features, tile_cols, counts, births, wq, wkv, wso, pos, wqkv, wo):
     snaps, rows, width = features.shape
-    smem = pl.BlockSpec(memory_space=pltpu.SMEM)
-    vmem = pl.BlockSpec(memory_space=pltpu.VMEM)
+    hbm = pl.BlockSpec(memory_space=pltpu.HBM)
     dma = pltpu.SemaphoreType.DMA
     half = jnp.bfloat16
     count = rows // RING
     result = pl.pallas_call(
         graph_kernel,
         out_shape=jax.ShapeDtypeStruct((RING * snaps, count, width), jnp.float32),
-        in_specs=[smem] * 3 + [vmem] * 7,
+        in_specs=[hbm] * 10,
         out_specs=pl.BlockSpec(memory_space=pl.ANY),
         scratch_shapes=[
+            pltpu.SMEM((rows // TILE, KT, snaps), jnp.int32),
+            pltpu.SMEM((rows // TILE, snaps), jnp.int32),
+            pltpu.SMEM(births.shape, jnp.int32),
+            pltpu.VMEM((BLOCKS, TILE, width), half),
+            pltpu.VMEM(wq.shape, half),
+            pltpu.VMEM(wkv.shape, half),
+            pltpu.VMEM(wso.shape, half),
+            pltpu.VMEM(pos.shape, half),
+            pltpu.VMEM(wqkv.shape, half),
+            pltpu.VMEM(wo.shape, half),
             pltpu.VMEM((17, 1, TILE), jnp.int32),
             pltpu.SMEM((17, 1, TILE), jnp.int32),
             pltpu.VMEM((8, 1, TILE), jnp.int32),
@@ -392,7 +422,7 @@
             pltpu.VMEM((BLOCKS, TILE, width), half),
             pltpu.VMEM((8, RING, RANKS, TILE, width), half),
             pltpu.VMEM((8, RING, RANKS, TILE, width), half),
-            pltpu.VMEM((BLOCKS, 2, TILE, TILE), half),
+            pltpu.VMEM((BLOCKS, width, width), half),
             pltpu.VMEM((4, width, width), half),
             pltpu.VMEM((2, RING * snaps * 8, RING * snaps * 8), half),
             pltpu.VMEM((SLOTS, width, TILE), jnp.float32),
@@ -402,13 +432,13 @@
             pltpu.VMEM((RING * snaps, count, width), half),
             pltpu.VMEM((RING, RING * snaps, 16, width), jnp.float32),
             dma((8,)), dma((8,)), dma, dma((3, 2)), dma((3, 2)),
-            dma((8, RING)), dma((8, RING)), dma((4, RING)), dma((4, RING)), dma, dma((4,)),
+            dma((8, RING)), dma((8, RING)), dma((4, RING)), dma((4, RING)), dma, dma((4,)), dma((10,)),
         ],
         compiler_params=pltpu.CompilerParams(
-            collective_id=0, has_side_effects=True, vmem_limit_bytes=56 * 2**20
+            collective_id=0, has_side_effects=True, vmem_limit_bytes=58 * 2**20
         ),
         name="graph",
-    )(tile_cols, counts, births, features.reshape(BLOCKS, TILE, width), wq, wkv, wso, pos, wqkv, wo)
+    )(tile_cols.transpose(1, 2, 0), counts.T, births, features.reshape(BLOCKS, TILE, width), wq, wkv, wso, pos, wqkv, wo)
     return result[:, None, None]
 
 

time: 96.8 us -> 88 us (0.909); the launches traced: 95.3 us -> 87.8 us
  Pallas kernels: 89.4 us -> 84.7 us
  local copies, waits for them, and re-layouts: 5.84 us -> 3.13 us
    pallas_call x1, Pallas kernels: 89.4 us -> 84.7 us  [local(): pl.pallas_call(graph_kernel, out_shape=jax.ShapeDtypeStruct((RING * snaps...]
    unnamed x3 -> x1, local copies, waits for them, and re-layouts: 5.84 us -> 3.13 us
where the time goes in v4:
time: 88 us; the launch traced here: 87.8 us
  Pallas kernels  84.7 us (96%)
  local copies, waits for them, and re-layouts  3.13 us (4%)
    pallas_call x1, Pallas kernels, local(): pl.pallas_call(graph_kernel, out_shape=jax.ShapeDtypeStruct((RING * snaps...  84.7 us
    unnamed x1, local copies, waits for them, and re-layouts  3.13 us

profile of v4, /device:TPU:0, one launch (start us, length us, event | category | flops | bytes accessed | tf_op | source)
XLA Modules:
  0.0 87.8 jit_solution(4381127628763809978)
XLA Ops:
  0.0 84.7 %graph.1 = f32[32,64,256]{2,1,0:T(8,128)} custom-call(s32[2,4,8]{2,1,0:T(4,128)} %bitcast.8, s32[2,8]{1,0:T(2,128)} %bitcast.9, s32[256]{0:T(256)} %births_in.1, bf16[16,128,256]{2,1,0:T(8,128)(2,1)} %bitcast.7, bf16[256,256]{1,0:T(8,128)(2,1)} %wq_hbm.1, bf16[256,512]{1,0:T(8,128)(2,1)} %wkv_hbm.1, bf16[256,256]{1,0:T(8,128)(2,1)} %wso_hbm.1, ...), custom_call_target="tpu_custom_call" | custom-call | tf_op jit(solution)/shard_map/graph/pallas_call | solution.py:400
  84.7 3.1 %copy.13 = f32[32,1,1,64,256]{4,3,2,1,0:T(8,128)} copy(f32[32,1,1,64,256]{4,3,2,1,0:T(8,128)} %bitcast.6) | data formatting | bytes 4194304

commit v5 on v4

--- a/solution.py
+++ b/solution.py
@@ -238,6 +238,10 @@
 
             attend3(row, j)
 
+    share(1, 0).wait_recv()
+    share(2, 0).start()
+    share(3, 1).wait_recv()
+    share(2, 1).start()
     for copy in held_here[2:]:
         copy.wait()
 
@@ -252,10 +256,6 @@
         wq[b, TILE:, :TILE] = jnp.zeros((TILE, TILE), jnp.bfloat16)
         wq[b, TILE:, TILE:] = q[TILE:]
 
-    share(1, 0).wait_recv()
-    share(2, 0).start()
-    share(3, 1).wait_recv()
-    share(2, 1).start()
     share(1, 1).wait_recv()
     share(3, 0).wait_recv()
     pass_on(0)
@@ -277,8 +277,7 @@
 
     attend_span(3, 32)
 
-    @pl.loop(0, 8)
-    def _(s):
+    def combine(s):
         for u in range(2):
             b = s * 2 + u
             slots, live, tops = [], [], []
@@ -308,20 +307,27 @@
             )
 
 
-    def spread(i, chunk):
+    def spread(i, chunk, half):
         group = (y + i) % RING
         return pltpu.make_async_remote_copy(
-            src_ref=hid.at[:, pl.ds(group * 64 + chunk * 16, 16)],
-            dst_ref=arr.at[pl.ds(y * 8, 8), pl.ds(chunk * 16, 16)],
-            send_sem=snap_send.at[chunk, i],
-            recv_sem=snap_recv.at[chunk, i],
+            src_ref=hid.at[pl.ds(half * 4, 4), pl.ds(group * 64 + chunk * 16, 16)],
+            dst_ref=arr.at[pl.ds(y * 8 + half * 4, 4), pl.ds(chunk * 16, 16)],
+            send_sem=snap_send.at[half, chunk, i],
+            recv_sem=snap_recv.at[half, chunk, i],
             device_id=(group, lax.axis_index("vert")),
             device_id_type=MESH,
         )
 
+    pl.loop(0, 4)(combine)
+    for chunk in range(2):
+        for i in (2, 1, 3):
+            spread(i, chunk, 0).start()
+    pl.loop(4, 8)(combine)
     for chunk in range(4):
-        for i in (2, 1, 3):
-            spread(i, chunk).start()
+        for half in range(2):
+            if half or chunk >= 2:
+                for i in (2, 1, 3):
+                    spread(i, chunk, half).start()
     arr[pl.ds(y * 8, 8)] = hid[:, pl.ds(y * 64, 64)]
 
     lane = lax.broadcasted_iota(jnp.int32, (1, 1, TILE), 2)
@@ -330,22 +336,31 @@
     own_lane = [lane // snaps == v for v in range(4)]
     positions = pos[...].astype(jnp.float32)[:, None, :]
 
+    vertex_of = [lax.broadcasted_iota(jnp.int32, (TILE, TILE), axis) // snaps for axis in range(2)]
+    same_vertex = (vertex_of[0] == vertex_of[1]).astype(jnp.float32).astype(jnp.bfloat16)
+
     def write(step):
         return pltpu.make_async_copy(held.at[step], out.at[:, pl.ds(step * 16, 16)], out_sem.at[step])
 
     @pl.loop(0, 4)
     def _(step):
         for i in range(1, RING):
-            spread(i, step).wait_recv()
+            for half in range(2):
+                spread(i, step, half).wait_recv()
         hidden = arr[:, pl.ds(step * 16, 16)].astype(jnp.float32)
+        groups = []
+        for g in range(2):
+            mine = hidden[:, g * 8 : (g + 1) * 8]
+            rows = (mine + positions).reshape(n, D).astype(jnp.bfloat16)
+            groups.append(dot(turn_s[0], rows).astype(jnp.bfloat16))
+        rows = jnp.concatenate(groups, axis=0)
+        q2 = (dot(wt[2], rows, NT) * SCALE).astype(jnp.bfloat16)
+        keys2 = dot(rows, wqkv[:, D : 2 * D]).astype(jnp.bfloat16)
+        values2 = dot(wt[3], rows, NT).astype(jnp.bfloat16)
         for g in range(2):
             base = y * 64 + step * 16 + g * 8
             mine = hidden[:, g * 8 : (g + 1) * 8]
-            rows = (mine + positions).reshape(n, D).astype(jnp.bfloat16)
-            rows = dot(turn_s[0], rows).astype(jnp.bfloat16)
-            q = (dot(wt[2], rows, NT) * SCALE).astype(jnp.bfloat16)
-            keys = dot(rows, wqkv[:, D : 2 * D]).astype(jnp.bfloat16)
-            values = dot(wt[3], rows, NT).astype(jnp.bfloat16)
+            q, keys, values = q2[:, g * n : (g + 1) * n], keys2[g * n : (g + 1) * n], values2[:, g * n : (g + 1) * n]
             sides = []
             for u in range(2):
                 birth = jnp.zeros((1, 1, TILE), jnp.int32)
@@ -365,14 +380,12 @@
                     near = near + bias
                     m = jnp.max(near, axis=1, keepdims=True)
                     e = jnp.exp2(near - m)
-                    t = jnp.sum(e, axis=1, keepdims=True)
+                    t = 1.0 / jnp.sum(e, axis=1, keepdims=True)
                     for h in range(4):
-                        wide = jnp.concatenate(
-                            [jnp.where(own_lane[v][0], e[h], 0.0) for v in range(4)], axis=0
-                        ).astype(jnp.bfloat16)
+                        wide = jnp.concatenate([e[h].astype(jnp.bfloat16)] * 4, axis=0) * same_vertex
                         top = (half * 4 + h) * HS
                         o = dot(values[top : top + HS, u * TILE : (u + 1) * TILE], wide)
-                        mixed.append((o / t[h]).astype(jnp.bfloat16))
+                        mixed.append((o * t[h]).astype(jnp.bfloat16))
                 sides.append(jnp.concatenate(mixed, axis=0))
             mixed = dot(turn_s[1], jnp.concatenate(sides, axis=1), NT).astype(jnp.bfloat16)
             held[step, :, g * 8 : (g + 1) * 8] = mine + dot(mixed, wo[...]).reshape(snaps, 8, D)
@@ -381,7 +394,8 @@
     for chunk in range(4):
         write(chunk).wait()
         for i in range(1, RING):
-            spread(i, chunk).wait_send()
+            for half in range(2):
+                spread(i, chunk, half).wait_send()
     for j, half in ((1, 0), (1, 1), (2, 0), (2, 1), (3, 0), (3, 1)):
         share(j, half).wait_send()
     for j in range(RING):
@@ -432,7 +446,7 @@
             pltpu.VMEM((RING * snaps, count, width), half),
             pltpu.VMEM((RING, RING * snaps, 16, width), jnp.float32),
             dma((8,)), dma((8,)), dma, dma((3, 2)), dma((3, 2)),
-            dma((8, RING)), dma((8, RING)), dma((4, RING)), dma((4, RING)), dma, dma((4,)), dma((10,)),
+            dma((8, RING)), dma((8, RING)), dma((2, 4, RING)), dma((2, 4, RING)), dma, dma((4,)), dma((10,)),
         ],
         compiler_params=pltpu.CompilerParams(
             collective_id=0, has_side_effects=True, vmem_limit_bytes=58 * 2**20

time: 88 us -> 86.2 us (0.980)
  Pallas kernels: 84.7 us -> 82.9 us
    pallas_call x1, Pallas kernels: 84.7 us -> 82.9 us  [local(): pl.pallas_call(graph_kernel, out_shape=jax.ShapeDtypeStruct((RING * snaps...]
where the time goes in v5:
time: 86.2 us; the launch traced here: 86.1 us
  Pallas kernels  82.9 us (96%)
  local copies, waits for them, and re-layouts  3.13 us (4%)
    pallas_call x1, Pallas kernels, local(): pl.pallas_call(graph_kernel, out_shape=jax.ShapeDtypeStruct((RING * snaps...  82.9 us
    unnamed x1, local copies, waits for them, and re-layouts  3.13 us

profile of v5, /device:TPU:0, one launch (start us, length us, event | category | flops | bytes accessed | tf_op | source)
XLA Modules:
  0.0 86.1 jit_solution(17708725031675344213)
XLA Ops:
  0.0 82.9 %graph.1 = f32[32,64,256]{2,1,0:T(8,128)} custom-call(s32[2,4,8]{2,1,0:T(4,128)} %bitcast.8, s32[2,8]{1,0:T(2,128)} %bitcast.9, s32[256]{0:T(256)} %births_in.1, bf16[16,128,256]{2,1,0:T(8,128)(2,1)} %bitcast.7, bf16[256,256]{1,0:T(8,128)(2,1)} %wq_hbm.1, bf16[256,512]{1,0:T(8,128)(2,1)} %wkv_hbm.1, bf16[256,256]{1,0:T(8,128)(2,1)} %wso_hbm.1, ...), custom_call_target="tpu_custom_call" | custom-call | tf_op jit(solution)/shard_map/graph/pallas_call | solution.py:414
  82.9 3.1 %copy.13 = f32[32,1,1,64,256]{4,3,2,1,0:T(8,128)} copy(f32[32,1,1,64,256]{4,3,2,1,0:T(8,128)} %bitcast.6) | data formatting | bytes 4194304
